TPU v7x, 32 devices: a whole 2x2x4 slice. The times are simulated.
32 devices in a mesh: out: 4 (over x, core), in: 8 (over z, y).
Axes of the slice: x: 2, y: 2, z: 4, core: 2. Of those that a mesh axis runs over, the one named last changes fastest.
Arguments:
- kernel_weights: bfloat16 [2, 4096, 8192], P(None, 'out', 'in'), may hold values from -0.0625 to 0.0625
- mode_field: bfloat16 [8192, 1024], P('in', 'out'), may hold values from -6 to 6
- diff_blocks: bfloat16 [2, 4096, 1024], P(None, 'out', 'in'), may hold values from -6 to 6
- block_table: int32 [4, 8], replicated, may hold values from 0 to 3, as said below
Outputs:
- gain: bfloat16 [4096, 1024], P('out', 'in')
Inputs may be any that keep to these rules, and one draw needn't show every extreme that they name: `block_table`: in every column the entries are 0 to 3, each once.
All inputs are finite; a program needn't handle non-finite values.
Results may differ from a plain program's by a relative error of at most 0.001.
Values may be sent and summed in bfloat16 or wider, within the bound.
No kernel may reach another device: no remote copies, remote signals or barrier semaphores. Data moves between devices by JAX's collectives and lax.ppermute only.
A program may use at most 64 MiB of HBM per device.

v0:
```python
import functools
import math

import jax
import jax.numpy as jnp
from jax import lax
from jax.experimental import pallas as pl
from jax.experimental.pallas import tpu as pltpu
from jax.sharding import PartitionSpec as P

PAIR = 2
TOP = 32767.0
GROUPS = 4
WEIGHTS = (4000, 50000)
KERNEL_MEMORY = 24 << 20
LANES = 128


def routed_shards(kernel_weights, mode_field, diff_blocks, block_table):
    out_index = lax.axis_index("out")
    tile_rows = kernel_weights.shape[1]
    term_count = kernel_weights.shape[0]
    own_cells = diff_blocks.shape[2]
    needed_row = block_table[out_index]
    whole_field = lax.all_gather(mode_field, "out", axis=1, tiled=True)
    every_block = lax.all_gather(diff_blocks, "out", axis=1, tiled=True)
    block_count = every_block.shape[1] // tile_rows
    every_block = every_block.reshape(term_count, block_count, tile_rows, own_cells)
    arranged = jnp.take(every_block, needed_row, axis=1)
    routed = lax.all_to_all(arranged, "in", split_axis=1, concat_axis=3, tiled=True)
    partial_value = jnp.zeros((tile_rows, whole_field.shape[1]), jnp.float32)
    for term_index in range(term_count):
        product = jnp.dot(kernel_weights[term_index], whole_field, preferred_element_type=jnp.float32)
        partial_value = partial_value + routed[term_index, 0].astype(jnp.float32) * product
    summed = lax.psum_scatter(partial_value, "in", scatter_dimension=1, tiled=True)
    return summed.astype(jnp.bfloat16)


def encode(values):
    largest = jnp.maximum(jnp.max(jnp.abs(values), axis=0, keepdims=True), 1e-30)
    exponent = jnp.floor(jnp.log2(largest)) + 1.0
    share = values * (jnp.exp2(-exponent) * (TOP * TOP))
    root = share * lax.rsqrt(jnp.abs(share) + 1e-9)
    return jnp.round(root).astype(jnp.int32), exponent.astype(jnp.int32)


def pack(high, low):
    return (high << 16) | (low & 0xFFFF)


def decode(codes, exponent):
    root = codes.astype(jnp.float32)
    return root * jnp.abs(root) * (jnp.exp2(exponent.astype(jnp.float32)) * (1.0 / (TOP * TOP)))


def unpack_high(packed, exponent):
    return decode(packed >> 16, exponent)


def unpack_low(packed, exponent):
    return decode((packed << 16) >> 16, exponent)


def position(index, out_index, chips):
    crossed = jnp.where(index % PAIR != out_index % PAIR, chips, 0)
    return crossed + (out_index // PAIR - index // PAIR + chips) % chips


def choose(index, refs, *at):
    value = refs[0][at]
    for place in range(1, len(refs)):
        value = jnp.where(index == place, refs[place][at], value)
    return value


def near(value):
    return pltpu.with_memory_space_constraint(value, pltpu.VMEM)


def kernel_call(kernel, name, inputs, in_table, outputs, scratch, flops, transcendentals):
    moved = sum(math.prod(array.shape) * jnp.dtype(array.dtype).itemsize for array in [*inputs, *outputs])
    memory = pl.BlockSpec(memory_space=pltpu.VMEM)
    return pl.pallas_call(
        kernel,
        name=name,
        out_shape=outputs,
        in_specs=[pl.BlockSpec(memory_space=pltpu.SMEM)] * in_table + [memory] * (len(inputs) - in_table),
        out_specs=[memory] * len(outputs),
        scratch_shapes=scratch,
        compiler_params=pltpu.CompilerParams(vmem_limit_bytes=KERNEL_MEMORY),
        cost_estimate=pl.CostEstimate(flops=4 * flops, bytes_accessed=4 * moved, transcendentals=transcendentals),
    )(*inputs)


def load_kernel(*refs):
    count = len(refs) // 2
    for source, place in zip(refs[:count], refs[count:]):
        place[...] = source[...]


def load(arrays):
    return kernel_call(
        load_kernel, "load", [near(array) for array in arrays], 0,
        [pltpu.VMEM(array.shape, array.dtype) for array in arrays], [], 0, 0,
    )


def multiply_kernel(shift, columns, weights, *refs):
    *fields, kept, sent, field = refs
    terms, total, _ = weights.shape
    rows = total // GROUPS
    half = kept.shape[2]
    in_index = lax.axis_index("in")
    target = (in_index // PAIR + shift) % columns
    source = position(target, lax.axis_index("out"), len(fields) // PAIR)
    side = in_index % PAIR

    for place, ref in enumerate(fields):
        for first in range(PAIR):
            @pl.when((source == place) & (side == first))
            def _():
                field[:, :half] = ref[:, first * half:(first + 1) * half]
                field[:, half:] = ref[:, (1 - first) * half:(2 - first) * half]

    for group in range(GROUPS):
        chosen = slice(group * rows, (group + 1) * rows)
        codes = []
        for term in range(terms):
            product = jnp.dot(weights[term, chosen], field[...], preferred_element_type=jnp.float32)
            kept[term, chosen] = product[:, :half]
            code, exponent = encode(product[:, half:])
            codes.append(code)
            place = total + term * GROUPS + group
            sent[place:place + 1, :] = exponent
        sent[chosen, :] = pack(*codes)


def multiply(shift, columns, weights, fields):
    terms, rows, depth = weights.shape
    width = fields[0].shape[1]
    half = width // PAIR
    return kernel_call(
        functools.partial(multiply_kernel, shift, columns),
        "products",
        [weights, *fields],
        0,
        [
            pltpu.VMEM((terms, rows, half), jnp.float32),
            pltpu.VMEM((rows + terms * GROUPS, half), jnp.int32),
        ],
        [pltpu.VMEM((depth, width), jnp.bfloat16)],
        2 * terms * rows * depth * width,
        rows * half * terms,
    )


def wanted_blocks(table, chips):
    out_index, in_index = lax.axis_index("out"), lax.axis_index("in")
    column, side = in_index // PAIR, in_index % PAIR
    return [position(table[out_index, column * PAIR + which], out_index, chips) for which in (side, 1 - side)]


def blocks_times_products(wanted, kept, received, pieces, rows):
    total = kept.shape[1]
    packed = received[rows, :]
    scale = total + rows.start // (total // GROUPS)
    mine = [kept[0, rows], kept[1, rows]]
    other = []
    for term, unpack in enumerate((unpack_high, unpack_low)):
        place = scale + term * GROUPS
        other.append(unpack(packed, received[place:place + 1, :]))
    value = None
    for index, products in zip(wanted, (mine, other)):
        for term, product in enumerate(products):
            chosen = choose(index, pieces, term, rows).astype(jnp.float32)
            value = chosen * product if value is None else value + chosen * product
    return value


def row_ranges(total):
    half = total // PAIR
    step = half // GROUPS
    return [
        [slice(part * half + group * step, part * half + (group + 1) * step) for part in range(PAIR)]
        for group in range(GROUPS)
    ]


def decode_kernel(coded, result):
    total = result.shape[0]
    for group, parts in enumerate(row_ranges(total)):
        for part, (rows, unpack) in enumerate(zip(parts, (unpack_high, unpack_low))):
            place = total // PAIR + part * GROUPS + group
            result[rows, :] = unpack(coded[parts[0], :], coded[place:place + 1, :])


def decoded_sums(coded, rows, weight):
    cells = coded.shape[1]
    return kernel_call(
        decode_kernel, "decoded_sums", [coded], 0, [pltpu.VMEM((rows, cells), jnp.float32)], [],
        weight * rows * cells, 0,
    )[0]


def sums_kernel(arrivals, table, kept, received, *refs):
    arrived, pieces, result = refs[:arrivals], refs[arrivals:-1], refs[-1]
    total = kept.shape[1]
    wanted = wanted_blocks(table, len(pieces) // PAIR)
    for group, parts in enumerate(row_ranges(total)):
        codes = []
        for part, (rows, unpack) in enumerate(zip(parts, (unpack_high, unpack_low))):
            value = blocks_times_products(wanted, kept, received, pieces, rows)
            place = total // PAIR + part * GROUPS + group
            for ref in arrived:
                value = value + ref[rows, :]
            if result.dtype == jnp.int32:
                code, exponent = encode(value)
                codes.append(code)
                result[place:place + 1, :] = exponent
            else:
                result[rows, :] = value.astype(result.dtype)
        if codes:
            result[parts[0], :] = pack(*codes)


def sums(name, table, kept, received, arrived, pieces, result):
    terms, rows, cells = kept.shape
    return kernel_call(
        functools.partial(sums_kernel, len(arrived)), name, [table, kept, received, *arrived, *pieces], 1,
        [result], [], 8 * terms * rows * cells, rows * cells,
    )[0]


def partial_sums(table, kept, received, arrived, pieces):
    terms, rows, cells = kept.shape
    result = pltpu.VMEM((rows // PAIR + PAIR * GROUPS, cells), jnp.int32)
    return sums("partial_sums", table, kept, received, arrived, pieces, result)


def final_sums(table, kept, received, arrived, pieces):
    terms, rows, cells = kept.shape
    result = jax.ShapeDtypeStruct((rows, cells), jnp.bfloat16)
    return sums("final_sums", table, kept, received, arrived, pieces, result)


def after(value, *earlier):
    return lax.optimization_barrier((value, *earlier))[0]


def gathered_shards(out_count, in_count, kernel_weights, mode_field, diff_blocks, block_table):
    columns = in_count // PAIR

    def across_cores(value):
        return lax.ppermute(value, "out", [(r, r ^ 1) for r in range(out_count)])

    def along_chips(value):
        return lax.ppermute(value, "out", [(r, (r + PAIR) % out_count) for r in range(out_count)])

    def across_sides(value):
        return lax.ppermute(value, "in", [(s, s ^ 1) for s in range(in_count)])

    def along_columns(value, shift):
        return lax.ppermute(value, "in", [(s, (s + PAIR * shift) % in_count) for s in range(in_count)])

    weights, own_field, own_blocks = load([kernel_weights, mode_field, diff_blocks])
    rings = [diff_blocks]
    for step in range(1, columns):
        rings.append(along_columns(rings[-1], -1))
    rings = rings[1:] + rings[:1]
    far_field = after(along_chips(mode_field), weights)
    core_field = after(across_cores(mode_field), rings[0])
    fields = [own_field] + [near(field) for field in (far_field, core_field, across_cores(far_field))]

    kept, received, sent = [], [], []
    for step in range(columns):
        products = multiply((step + 1) % columns, columns, weights, fields)
        kept.append(products[0])
        sent.append(products[1])
        received.append(near(across_sides(after(products[1], *received[-1:]))))
    core_own = across_cores(diff_blocks)

    arrived, ahead = [], sent
    for step in range(columns):
        last = step == columns - 1
        waits = [far_field] if step == 0 else rings[columns - 2:columns - 1] if last else []
        far = along_chips(after(rings[step], *waits))
        pieces = [own_blocks if last else near(rings[step]), near(far)]
        pieces += [near(core_own if last else across_cores(after(rings[step], *ahead))), near(across_cores(after(far, *ahead)))]
        if last:
            return final_sums(block_table, kept[step], received[step], arrived, pieces)
        total = partial_sums(block_table, kept[step], received[step], arrived, pieces)
        coming = near(along_columns(total, -1))
        arrived = [decoded_sums(coming, kernel_weights.shape[1], WEIGHTS[step == columns - 2])]
        ahead = [total, *([core_own] if step == 0 else [])]


def solution(mesh):
    out_count, in_count = mesh.shape["out"], mesh.shape["in"]
    in_specs = (P(None, "out", "in"), P("in", "out"), P(None, "out", "in"), P())
    out_specs = P("out", "in")

    def shards(kernel_weights, mode_field, diff_blocks, block_table):
        own_cells = diff_blocks.shape[2]
        gather = (
            kernel_weights.shape[0] == PAIR
            and own_cells % LANES == 0
            and mode_field.shape[1] == PAIR * own_cells
            and out_count == PAIR * PAIR
            and in_count == PAIR * out_count
        )
        if gather:
            return gathered_shards(out_count, in_count, kernel_weights, mode_field, diff_blocks, block_table)
        return routed_shards(kernel_weights, mode_field, diff_blocks, block_table)

    return jax.shard_map(shards, mesh=mesh, in_specs=in_specs, out_specs=out_specs, check_vma=False)
```

profile of v0, /device:TPU:0, one launch (start us, length us, event | category | flops | bytes accessed | tf_op | source)
XLA Modules:
  0.0 92.8 jit_solution(17486233556108286270)
XLA Ops:
  0.0 2.9 %collective-permute-start = (bf16[1024,256]{1,0:T(8,128)(2,1)}, bf16[1024,256]{1,0:T(8,128)(2,1)S(1)}, u32[]{:S(2)}, u32[]{:S(2)}) collective-permute-start(bf16[1024,256]{1,0:T(8,128)(2,1)} %refs_1_.1), channel_id=1, source_target_pairs={{0,16},{8,24},{16,0},{24,8},{1,17},{9,25},{17,1},{25,9},{2,18},{10... | collective-permute-start | bytes 1572872 | tf_op jit(solution)/shard_map/ppermute | solution.py:257
  2.9 3.6 %collective-permute-start.2 = (bf16[2,1024,128]{2,1,0:T(8,128)(2,1)}, bf16[2,1024,128]{2,1,0:T(8,128)(2,1)S(1)}, u32[]{:S(2)}, u32[]{:S(2)}) collective-permute-start(bf16[2,1024,128]{2,1,0:T(8,128)(2,1)} %refs_2_.1), channel_id=1, source_target_pairs={{0,6},{1,7},{2,0},{3,1},{4,2},{5,3},{6,4},{7,5},{8,14},{9,15},{10,... | collective-permute-start | bytes 1572872 | tf_op jit(solution)/shard_map/ppermute | solution.py:263
  6.5 2.2 %copy-done = bf16[2,1024,1024]{2,1,0:T(8,128)(2,1)S(1)} copy-done((bf16[2,1024,1024]{2,1,0:T(8,128)(2,1)S(1)}, bf16[2,1024,1024]{2,1,0:T(8,128)(2,1)}, u32[]{:S(2)}) %copy-start) | copy-done | bytes 4194328
  11.2 3.9 %collective-permute-done.refs_1_ = bf16[1024,256]{1,0:T(8,128)(2,1)S(1)} collective-permute-done((bf16[1024,256]{1,0:T(8,128)(2,1)}, bf16[1024,256]{1,0:T(8,128)(2,1)S(1)}, u32[]{:S(2)}, u32[]{:S(2)}) %collective-permute-start) | collective-permute-done | bytes 524320 | tf_op jit(solution)/shard_map/ppermute | solution.py:257
  15.1 3.6 %collective-permute-done.2.refs_0_ = bf16[2,1024,128]{2,1,0:T(8,128)(2,1)S(1)} collective-permute-done((bf16[2,1024,128]{2,1,0:T(8,128)(2,1)}, bf16[2,1024,128]{2,1,0:T(8,128)(2,1)S(1)}, u32[]{:S(2)}, u32[]{:S(2)}) %collective-permute-start.2) | collective-permute-done | bytes 524320 | tf_op jit(solution)/shard_map/ppermute | solution.py:263
  19.3 4.2 %collective-permute-start.12 = (bf16[2,1024,128]{2,1,0:T(8,128)(2,1)S(1)}, bf16[2,1024,128]{2,1,0:T(8,128)(2,1)S(1)}, u32[]{:S(2)}, u32[]{:S(2)}) collective-permute-start(bf16[2,1024,128]{2,1,0:T(8,128)(2,1)S(1)} %collective-permute-done.2.refs_0_), channel_id=1, source_target_pairs={{0,6},{1,7},{2,0},{3,1},{4,2},{5,3},{6,4},{7,5},{8,14},{9,15},{10,... | collective-permute-start | bytes 1572872 | tf_op jit(solution)/shard_map/ppermute | solution.py:263
  23.4 1.5 %products.7 = (f32[2,1024,128]{2,1,0:T(8,128)S(1)}, s32[1032,128]{1,0:T(8,128)S(1)}) custom-call(bf16[2,1024,1024]{2,1,0:T(8,128)(2,1)S(1)} %get-tuple-element.30.weights, bf16[1024,256]{1,0:T(8,128)(2,1)S(1)} %get-tuple-element.31.refs_0_, bf16[1024,256]{1,0:T(8,128)(2,1)S(1)} %collective-permute-done.refs_1_, ...), custom_call_target="tpu_custom_call" | custom-call | flops 4294967296 | bytes 31473664 | tf_op jit(solution)/shard_map/products/pallas_call | solution.py:83
  25.0 1.6 %collective-permute-start.4 = (s32[1032,128]{1,0:T(8,128)S(1)}, s32[1032,128]{1,0:T(8,128)S(1)}, u32[]{:S(2)}, u32[]{:S(2)}) collective-permute-start(s32[1032,128]{1,0:T(8,128)S(1)} %get-tuple-element.38), channel_id=1, source_target_pairs={{0,1},{1,0},{2,3},{3,2},{4,5},{5,4},{6,7},{7,6},{8,9},{9,8},{10,11... | collective-permute-start | bytes 1585160 | tf_op jit(solution)/shard_map/ppermute | solution.py:260
  26.6 1.5 %products.4 = (f32[2,1024,128]{2,1,0:T(8,128)S(1)}, s32[1032,128]{1,0:T(8,128)S(1)}) custom-call(bf16[2,1024,1024]{2,1,0:T(8,128)(2,1)S(1)} %get-tuple-element.30.weights, bf16[1024,256]{1,0:T(8,128)(2,1)S(1)} %get-tuple-element.31.refs_0_, bf16[1024,256]{1,0:T(8,128)(2,1)S(1)} %collective-permute-done.refs_1_, ...), custom_call_target="tpu_custom_call" | custom-call | flops 4294967296 | bytes 31473664 | tf_op jit(solution)/shard_map/products/pallas_call | solution.py:83
  28.1 1.6 %products.5 = (f32[2,1024,128]{2,1,0:T(8,128)S(1)}, s32[1032,128]{1,0:T(8,128)S(1)}) custom-call(bf16[2,1024,1024]{2,1,0:T(8,128)(2,1)S(1)} %get-tuple-element.30.weights, bf16[1024,256]{1,0:T(8,128)(2,1)S(1)} %get-tuple-element.31.refs_0_, bf16[1024,256]{1,0:T(8,128)(2,1)S(1)} %collective-permute-done.refs_1_, ...), custom_call_target="tpu_custom_call" | custom-call | flops 4294967296 | bytes 31473664 | tf_op jit(solution)/shard_map/products/pallas_call | solution.py:83
  29.8 1.6 %products.6 = (f32[2,1024,128]{2,1,0:T(8,128)S(1)}, s32[1032,128]{1,0:T(8,128)S(1)}) custom-call(bf16[2,1024,1024]{2,1,0:T(8,128)(2,1)S(1)} %get-tuple-element.30.weights, bf16[1024,256]{1,0:T(8,128)(2,1)S(1)} %get-tuple-element.31.refs_0_, bf16[1024,256]{1,0:T(8,128)(2,1)S(1)} %collective-permute-done.refs_1_, ...), custom_call_target="tpu_custom_call" | custom-call | flops 4294967296 | bytes 31473664 | tf_op jit(solution)/shard_map/products/pallas_call | solution.py:83
  35.7 2.4 %collective-permute-done.4.received = s32[1032,128]{1,0:T(8,128)S(1)} collective-permute-done((s32[1032,128]{1,0:T(8,128)S(1)}, s32[1032,128]{1,0:T(8,128)S(1)}, u32[]{:S(2)}, u32[]{:S(2)}) %collective-permute-start.4) | collective-permute-done | bytes 528416 | tf_op jit(solution)/shard_map/ppermute | solution.py:260
  38.1 1.9 %collective-permute-start.18 = (bf16[2,1024,128]{2,1,0:T(8,128)(2,1)S(1)}, bf16[2,1024,128]{2,1,0:T(8,128)(2,1)S(1)}, u32[]{:S(2)}, u32[]{:S(2)}) collective-permute-start(bf16[2,1024,128]{2,1,0:T(8,128)(2,1)S(1)} %collective-permute-done.12.refs_1_), channel_id=1, source_target_pairs={{0,6},{1,7},{2,0},{3,1},{4,2},{5,3},{6,4},{7,5},{8,14},{9,15},{10,... | collective-permute-start | bytes 1572872 | tf_op jit(solution)/shard_map/ppermute | solution.py:263
  43.1 3.6 %collective-permute-done.13.refs_2_ = bf16[2,1024,128]{2,1,0:T(8,128)(2,1)S(1)} collective-permute-done((bf16[2,1024,128]{2,1,0:T(8,128)(2,1)S(1)}, bf16[2,1024,128]{2,1,0:T(8,128)(2,1)S(1)}, u32[]{:S(2)}, u32[]{:S(2)}) %collective-permute-start.13) | collective-permute-done | bytes 524320 | tf_op jit(solution)/shard_map/ppermute | solution.py:257
  46.7 3.5 %collective-permute-done.18.refs_1_ = bf16[2,1024,128]{2,1,0:T(8,128)(2,1)S(1)} collective-permute-done((bf16[2,1024,128]{2,1,0:T(8,128)(2,1)S(1)}, bf16[2,1024,128]{2,1,0:T(8,128)(2,1)S(1)}, u32[]{:S(2)}, u32[]{:S(2)}) %collective-permute-start.18) | collective-permute-done | bytes 524320 | tf_op jit(solution)/shard_map/ppermute | solution.py:263
  51.7 2.7 %collective-permute-start.11 = (s32[520,128]{1,0:T(8,128)S(1)}, s32[520,128]{1,0:T(8,128)S(1)}, u32[]{:S(2)}, u32[]{:S(2)}) collective-permute-start(s32[520,128]{1,0:T(8,128)S(1)} %partial_sums.3), channel_id=1, source_target_pairs={{0,6},{1,7},{2,0},{3,1},{4,2},{5,3},{6,4},{7,5},{8,14},{9,15},{10,... | collective-permute-start | bytes 798728 | tf_op jit(solution)/shard_map/ppermute | solution.py:263
  55.9 2.5 %collective-permute-done.11.coded = s32[520,128]{1,0:T(8,128)S(1)} collective-permute-done((s32[520,128]{1,0:T(8,128)S(1)}, s32[520,128]{1,0:T(8,128)S(1)}, u32[]{:S(2)}, u32[]{:S(2)}) %collective-permute-start.11) | collective-permute-done | bytes 266272 | tf_op jit(solution)/shard_map/ppermute | solution.py:263
  61.4 3.8 %collective-permute-start.17 = (s32[520,128]{1,0:T(8,128)S(1)}, s32[520,128]{1,0:T(8,128)S(1)}, u32[]{:S(2)}, u32[]{:S(2)}) collective-permute-start(s32[520,128]{1,0:T(8,128)S(1)} %partial_sums.4), channel_id=1, source_target_pairs={{0,6},{1,7},{2,0},{3,1},{4,2},{5,3},{6,4},{7,5},{8,14},{9,15},{10,... | collective-permute-start | bytes 798728 | tf_op jit(solution)/shard_map/ppermute | solution.py:263
  66.7 4.8 %collective-permute-done.17.coded = s32[520,128]{1,0:T(8,128)S(1)} collective-permute-done((s32[520,128]{1,0:T(8,128)S(1)}, s32[520,128]{1,0:T(8,128)S(1)}, u32[]{:S(2)}, u32[]{:S(2)}) %collective-permute-start.17) | collective-permute-done | bytes 266272 | tf_op jit(solution)/shard_map/ppermute | solution.py:263
  71.7 1.5 %partial_sums.5 = s32[520,128]{1,0:T(8,128)S(1)} custom-call(s32[4,8]{1,0:T(4,128)S(1)} %copy-done.4, f32[2,1024,128]{2,1,0:T(8,128)S(1)} %get-tuple-element.42.kept, s32[1032,128]{1,0:T(8,128)S(1)} %collective-permute-done.6.received, f32[1024,128]{1,0:T(8,128)S(1)} %decoded_sums.4.refs_0_, bf16[2,1024,128]{2,1,0:T(8,128)(2,1)S(1)} %collective-permute-done.18.refs_1_, ...), custom_call_target="tpu_custom_call" | custom-call | flops 8388608 | bytes 17859072 | tf_op jit(solution)/shard_map/partial_sums/pallas_call | solution.py:83
  73.2 4.3 %collective-permute-start.22 = (s32[520,128]{1,0:T(8,128)S(1)}, s32[520,128]{1,0:T(8,128)S(1)}, u32[]{:S(2)}, u32[]{:S(2)}) collective-permute-start(s32[520,128]{1,0:T(8,128)S(1)} %partial_sums.5), channel_id=1, source_target_pairs={{0,6},{1,7},{2,0},{3,1},{4,2},{5,3},{6,4},{7,5},{8,14},{9,15},{10,... | collective-permute-start | bytes 798728 | tf_op jit(solution)/shard_map/ppermute | solution.py:263
  79.3 3.8 %collective-permute-done.22.coded = s32[520,128]{1,0:T(8,128)S(1)} collective-permute-done((s32[520,128]{1,0:T(8,128)S(1)}, s32[520,128]{1,0:T(8,128)S(1)}, u32[]{:S(2)}, u32[]{:S(2)}) %collective-permute-start.22) | collective-permute-done | bytes 266272 | tf_op jit(solution)/shard_map/ppermute | solution.py:263
  83.2 7.7 %collective-permute-done.7.received = s32[1032,128]{1,0:T(8,128)S(1)} collective-permute-done((s32[1032,128]{1,0:T(8,128)S(1)}, s32[1032,128]{1,0:T(8,128)S(1)}, u32[]{:S(2)}, u32[]{:S(2)}) %collective-permute-start.7) | collective-permute-done | bytes 528416 | tf_op jit(solution)/shard_map/ppermute | solution.py:260
  90.9 1.9 %final_sums.1 = bf16[1024,128]{1,0:T(8,128)(2,1)} custom-call(s32[4,8]{1,0:T(4,128)S(1)} %copy-done.4, f32[2,1024,128]{2,1,0:T(8,128)S(1)} %get-tuple-element.34.kept, s32[1032,128]{1,0:T(8,128)S(1)} %collective-permute-done.7.received, f32[1024,128]{1,0:T(8,128)S(1)} %decoded_sums.5.refs_0_, bf16[2,1024,128]{2,1,0:T(8,128)(2,1)S(1)} %get-tuple-element.52.refs_1_, ...), custom_call_target="tpu_custom_call" | custom-call | flops 8388608 | bytes 17842688 | tf_op jit(solution)/shard_map/final_sums/pallas_call | solution.py:83
  (48 shorter events, 19.8 us)
Async XLA Ops:
  0.0 15.1 %collective-permute-start = (bf16[1024,256]{1,0:T(8,128)(2,1)}, bf16[1024,256]{1,0:T(8,128)(2,1)S(1)}, u32[]{:S(2)}, u32[]{:S(2)}) collective-permute-start(bf16[1024,256]{1,0:T(8,128)(2,1)} %refs_1_.1), channel_id=1, source_target_pairs={{0,16},{8,24},{16,0},{24,8},{1,17},{9,25},{17,1},{25,9},{2,18},{10... | collective-permute-start | bytes 1572872 | tf_op jit(solution)/shard_map/ppermute | solution.py:257
  2.9 12.1 %collective-permute-start.1 = (bf16[1024,256]{1,0:T(8,128)(2,1)}, bf16[1024,256]{1,0:T(8,128)(2,1)S(1)}, u32[]{:S(2)}, u32[]{:S(2)}) collective-permute-start(bf16[1024,256]{1,0:T(8,128)(2,1)} %refs_1_.1), channel_id=1, source_target_pairs={{0,8},{8,0},{16,24},{24,16},{1,9},{9,1},{17,25},{25,17},{2,10},{10... | collective-permute-start | bytes 1572872 | tf_op jit(solution)/shard_map/ppermute | solution.py:254
  2.9 15.8 %collective-permute-start.2 = (bf16[2,1024,128]{2,1,0:T(8,128)(2,1)}, bf16[2,1024,128]{2,1,0:T(8,128)(2,1)S(1)}, u32[]{:S(2)}, u32[]{:S(2)}) collective-permute-start(bf16[2,1024,128]{2,1,0:T(8,128)(2,1)} %refs_2_.1), channel_id=1, source_target_pairs={{0,6},{1,7},{2,0},{3,1},{4,2},{5,3},{6,4},{7,5},{8,14},{9,15},{10,... | collective-permute-start | bytes 1572872 | tf_op jit(solution)/shard_map/ppermute | solution.py:263
  15.1 8.4 %collective-permute-start.3 = (bf16[1024,256]{1,0:T(8,128)(2,1)S(1)}, bf16[1024,256]{1,0:T(8,128)(2,1)S(1)}, u32[]{:S(2)}, u32[]{:S(2)}) collective-permute-start(bf16[1024,256]{1,0:T(8,128)(2,1)S(1)} %collective-permute-done.refs_1_), channel_id=1, source_target_pairs={{0,8},{8,0},{16,24},{24,16},{1,9},{9,1},{17,25},{25,17},{2,10},{10... | collective-permute-start | bytes 1572872 | tf_op jit(solution)/shard_map/ppermute | solution.py:254
  18.7 13.6 %collective-permute-start.8 = (bf16[2,1024,128]{2,1,0:T(8,128)(2,1)S(1)}, bf16[2,1024,128]{2,1,0:T(8,128)(2,1)S(1)}, u32[]{:S(2)}, u32[]{:S(2)}) collective-permute-start(bf16[2,1024,128]{2,1,0:T(8,128)(2,1)S(1)} %collective-permute-done.2.refs_0_), channel_id=1, source_target_pairs={{0,16},{8,24},{16,0},{24,8},{1,17},{9,25},{17,1},{25,9},{2,18},{10... | collective-permute-start | bytes 1572872 | tf_op jit(solution)/shard_map/ppermute | solution.py:257
  19.3 15.0 %collective-permute-start.12 = (bf16[2,1024,128]{2,1,0:T(8,128)(2,1)S(1)}, bf16[2,1024,128]{2,1,0:T(8,128)(2,1)S(1)}, u32[]{:S(2)}, u32[]{:S(2)}) collective-permute-start(bf16[2,1024,128]{2,1,0:T(8,128)(2,1)S(1)} %collective-permute-done.2.refs_0_), channel_id=1, source_target_pairs={{0,6},{1,7},{2,0},{3,1},{4,2},{5,3},{6,4},{7,5},{8,14},{9,15},{10,... | collective-permute-start | bytes 1572872 | tf_op jit(solution)/shard_map/ppermute | solution.py:263
  25.0 13.2 %collective-permute-start.4 = (s32[1032,128]{1,0:T(8,128)S(1)}, s32[1032,128]{1,0:T(8,128)S(1)}, u32[]{:S(2)}, u32[]{:S(2)}) collective-permute-start(s32[1032,128]{1,0:T(8,128)S(1)} %get-tuple-element.38), channel_id=1, source_target_pairs={{0,1},{1,0},{2,3},{3,2},{4,5},{5,4},{6,7},{7,6},{8,9},{9,8},{10,11... | collective-permute-start | bytes 1585160 | tf_op jit(solution)/shard_map/ppermute | solution.py:260
  31.4 8.6 %collective-permute-start.9 = (bf16[2,1024,128]{2,1,0:T(8,128)(2,1)S(1)}, bf16[2,1024,128]{2,1,0:T(8,128)(2,1)S(1)}, u32[]{:S(2)}, u32[]{:S(2)}) collective-permute-start(bf16[2,1024,128]{2,1,0:T(8,128)(2,1)S(1)} %collective-permute-done.2.refs_0_), channel_id=1, source_target_pairs={{0,8},{8,0},{16,24},{24,16},{1,9},{9,1},{17,25},{25,17},{2,10},{10... | collective-permute-start | bytes 1572872 | tf_op jit(solution)/shard_map/ppermute | solution.py:254
  32.3 9.2 %collective-permute-start.10 = (bf16[2,1024,128]{2,1,0:T(8,128)(2,1)S(1)}, bf16[2,1024,128]{2,1,0:T(8,128)(2,1)S(1)}, u32[]{:S(2)}, u32[]{:S(2)}) collective-permute-start(bf16[2,1024,128]{2,1,0:T(8,128)(2,1)S(1)} %collective-permute-done.8.refs_1_), channel_id=1, source_target_pairs={{0,8},{8,0},{16,24},{24,16},{1,9},{9,1},{17,25},{25,17},{2,10},{10... | collective-permute-start | bytes 1572872 | tf_op jit(solution)/shard_map/ppermute | solution.py:254
  32.3 10.7 %collective-permute-start.14 = (bf16[2,1024,128]{2,1,0:T(8,128)(2,1)S(1)}, bf16[2,1024,128]{2,1,0:T(8,128)(2,1)S(1)}, u32[]{:S(2)}, u32[]{:S(2)}) collective-permute-start(bf16[2,1024,128]{2,1,0:T(8,128)(2,1)S(1)} %copy-done.3), channel_id=1, source_target_pairs={{0,8},{8,0},{16,24},{24,16},{1,9},{9,1},{17,25},{25,17},{2,10},{10... | collective-permute-start | bytes 1572872 | tf_op jit(solution)/shard_map/ppermute | solution.py:254
  34.2 12.5 %collective-permute-start.13 = (bf16[2,1024,128]{2,1,0:T(8,128)(2,1)S(1)}, bf16[2,1024,128]{2,1,0:T(8,128)(2,1)S(1)}, u32[]{:S(2)}, u32[]{:S(2)}) collective-permute-start(bf16[2,1024,128]{2,1,0:T(8,128)(2,1)S(1)} %collective-permute-done.12.refs_1_), channel_id=1, source_target_pairs={{0,16},{8,24},{16,0},{24,8},{1,17},{9,25},{17,1},{25,9},{2,18},{10... | collective-permute-start | bytes 1572872 | tf_op jit(solution)/shard_map/ppermute | solution.py:257
  38.1 12.1 %collective-permute-start.18 = (bf16[2,1024,128]{2,1,0:T(8,128)(2,1)S(1)}, bf16[2,1024,128]{2,1,0:T(8,128)(2,1)S(1)}, u32[]{:S(2)}, u32[]{:S(2)}) collective-permute-start(bf16[2,1024,128]{2,1,0:T(8,128)(2,1)S(1)} %collective-permute-done.12.refs_1_), channel_id=1, source_target_pairs={{0,6},{1,7},{2,0},{3,1},{4,2},{5,3},{6,4},{7,5},{8,14},{9,15},{10,... | collective-permute-start | bytes 1572872 | tf_op jit(solution)/shard_map/ppermute | solution.py:263
  40.0 14.4 %collective-permute-start.5 = (s32[1032,128]{1,0:T(8,128)S(1)}, s32[1032,128]{1,0:T(8,128)S(1)}, u32[]{:S(2)}, u32[]{:S(2)}) collective-permute-start(s32[1032,128]{1,0:T(8,128)S(1)} %get-tuple-element.39), channel_id=1, source_target_pairs={{0,1},{1,0},{2,3},{3,2},{4,5},{5,4},{6,7},{7,6},{8,9},{9,8},{10,11... | collective-permute-start | bytes 1585160 | tf_op jit(solution)/shard_map/ppermute | solution.py:260
  43.0 15.5 %collective-permute-start.15 = (bf16[2,1024,128]{2,1,0:T(8,128)(2,1)S(1)}, bf16[2,1024,128]{2,1,0:T(8,128)(2,1)S(1)}, u32[]{:S(2)}, u32[]{:S(2)}) collective-permute-start(bf16[2,1024,128]{2,1,0:T(8,128)(2,1)S(1)} %collective-permute-done.12.refs_1_), channel_id=1, source_target_pairs={{0,8},{8,0},{16,24},{24,16},{1,9},{9,1},{17,25},{25,17},{2,10},{10... | collective-permute-start | bytes 1572872 | tf_op jit(solution)/shard_map/ppermute | solution.py:254
  46.7 11.8 %collective-permute-start.16 = (bf16[2,1024,128]{2,1,0:T(8,128)(2,1)S(1)}, bf16[2,1024,128]{2,1,0:T(8,128)(2,1)S(1)}, u32[]{:S(2)}, u32[]{:S(2)}) collective-permute-start(bf16[2,1024,128]{2,1,0:T(8,128)(2,1)S(1)} %collective-permute-done.13.refs_2_), channel_id=1, source_target_pairs={{0,8},{8,0},{16,24},{24,16},{1,9},{9,1},{17,25},{25,17},{2,10},{10... | collective-permute-start | bytes 1572872 | tf_op jit(solution)/shard_map/ppermute | solution.py:254
  50.2 11.2 %collective-permute-start.19 = (bf16[2,1024,128]{2,1,0:T(8,128)(2,1)S(1)}, bf16[2,1024,128]{2,1,0:T(8,128)(2,1)S(1)}, u32[]{:S(2)}, u32[]{:S(2)}) collective-permute-start(bf16[2,1024,128]{2,1,0:T(8,128)(2,1)S(1)} %collective-permute-done.18.refs_1_), channel_id=1, source_target_pairs={{0,16},{8,24},{16,0},{24,8},{1,17},{9,25},{17,1},{25,9},{2,18},{10... | collective-permute-start | bytes 1572872 | tf_op jit(solution)/shard_map/ppermute | solution.py:257
  51.7 6.7 %collective-permute-start.11 = (s32[520,128]{1,0:T(8,128)S(1)}, s32[520,128]{1,0:T(8,128)S(1)}, u32[]{:S(2)}, u32[]{:S(2)}) collective-permute-start(s32[520,128]{1,0:T(8,128)S(1)} %partial_sums.3), channel_id=1, source_target_pairs={{0,6},{1,7},{2,0},{3,1},{4,2},{5,3},{6,4},{7,5},{8,14},{9,15},{10,... | collective-permute-start | bytes 798728 | tf_op jit(solution)/shard_map/ppermute | solution.py:263
  54.4 17.2 %collective-permute-start.6 = (s32[1032,128]{1,0:T(8,128)S(1)}, s32[1032,128]{1,0:T(8,128)S(1)}, u32[]{:S(2)}, u32[]{:S(2)}) collective-permute-start(s32[1032,128]{1,0:T(8,128)S(1)} %get-tuple-element.40), channel_id=1, source_target_pairs={{0,1},{1,0},{2,3},{3,2},{4,5},{5,4},{6,7},{7,6},{8,9},{9,8},{10,11... | collective-permute-start | bytes 1585160 | tf_op jit(solution)/shard_map/ppermute | solution.py:260
  60.0 11.6 %collective-permute-start.20 = (bf16[2,1024,128]{2,1,0:T(8,128)(2,1)S(1)}, bf16[2,1024,128]{2,1,0:T(8,128)(2,1)S(1)}, u32[]{:S(2)}, u32[]{:S(2)}) collective-permute-start(bf16[2,1024,128]{2,1,0:T(8,128)(2,1)S(1)} %collective-permute-done.18.refs_1_), channel_id=1, source_target_pairs={{0,8},{8,0},{16,24},{24,16},{1,9},{9,1},{17,25},{25,17},{2,10},{10... | collective-permute-start | bytes 1572872 | tf_op jit(solution)/shard_map/ppermute | solution.py:254
  61.4 10.2 %collective-permute-start.21 = (bf16[2,1024,128]{2,1,0:T(8,128)(2,1)S(1)}, bf16[2,1024,128]{2,1,0:T(8,128)(2,1)S(1)}, u32[]{:S(2)}, u32[]{:S(2)}) collective-permute-start(bf16[2,1024,128]{2,1,0:T(8,128)(2,1)S(1)} %collective-permute-done.19.refs_2_), channel_id=1, source_target_pairs={{0,8},{8,0},{16,24},{24,16},{1,9},{9,1},{17,25},{25,17},{2,10},{10... | collective-permute-start | bytes 1572872 | tf_op jit(solution)/shard_map/ppermute | solution.py:254
  61.4 10.1 %collective-permute-start.17 = (s32[520,128]{1,0:T(8,128)S(1)}, s32[520,128]{1,0:T(8,128)S(1)}, u32[]{:S(2)}, u32[]{:S(2)}) collective-permute-start(s32[520,128]{1,0:T(8,128)S(1)} %partial_sums.4), channel_id=1, source_target_pairs={{0,6},{1,7},{2,0},{3,1},{4,2},{5,3},{6,4},{7,5},{8,14},{9,15},{10,... | collective-permute-start | bytes 798728 | tf_op jit(solution)/shard_map/ppermute | solution.py:263
  65.2 14.1 %collective-permute-start.23 = (bf16[2,1024,128]{2,1,0:T(8,128)(2,1)S(1)}, bf16[2,1024,128]{2,1,0:T(8,128)(2,1)S(1)}, u32[]{:S(2)}, u32[]{:S(2)}) collective-permute-start(bf16[2,1024,128]{2,1,0:T(8,128)(2,1)S(1)} %copy-done.3), channel_id=1, source_target_pairs={{0,16},{8,24},{16,0},{24,8},{1,17},{9,25},{17,1},{25,9},{2,18},{10... | collective-permute-start | bytes 1572872 | tf_op jit(solution)/shard_map/ppermute | solution.py:257
  73.2 9.9 %collective-permute-start.22 = (s32[520,128]{1,0:T(8,128)S(1)}, s32[520,128]{1,0:T(8,128)S(1)}, u32[]{:S(2)}, u32[]{:S(2)}) collective-permute-start(s32[520,128]{1,0:T(8,128)S(1)} %partial_sums.5), channel_id=1, source_target_pairs={{0,6},{1,7},{2,0},{3,1},{4,2},{5,3},{6,4},{7,5},{8,14},{9,15},{10,... | collective-permute-start | bytes 798728 | tf_op jit(solution)/shard_map/ppermute | solution.py:263
  77.5 13.4 %collective-permute-start.7 = (s32[1032,128]{1,0:T(8,128)S(1)}, s32[1032,128]{1,0:T(8,128)S(1)}, u32[]{:S(2)}, u32[]{:S(2)}) collective-permute-start(s32[1032,128]{1,0:T(8,128)S(1)} %get-tuple-element.41), channel_id=1, source_target_pairs={{0,1},{1,0},{2,3},{3,2},{4,5},{5,4},{6,7},{7,6},{8,9},{9,8},{10,11... | collective-permute-start | bytes 1585160 | tf_op jit(solution)/shard_map/ppermute | solution.py:260
  (6 other events, 22.5 us)
where the time goes:
time: 93.1 us; the launch traced here: 92.8 us
  waiting for transfers between devices  39.7 us (43%)
  starting transfers between devices  35.3 us (38%)
  Pallas kernels  13.3 us (14%)
  local copies, waits for them, and re-layouts  4.28 us (5%)
    ppermute x6, starting transfers between devices, along_columns(): lax.ppermute(value, 'in', [(s, (s + PAIR * shift) % in_count) for s in ra...  20.5 us
    ppermute x6, waiting for transfers between devices, along_columns(): lax.ppermute(value, 'in', [(s, (s + PAIR * shift) % in_count) for s in ra...  19.7 us
    pallas_call x12, Pallas kernels, kernel_call(): pl.pallas_call(kernel, name=name, out_shape=outputs, in_specs=[pl.BlockSp...  13.3 us
    ppermute x4, waiting for transfers between devices, across_sides(): return lax.ppermute(value, 'in', [(s, s ^ 1) for s in range(in_count)])  10.1 us
    ppermute x5, waiting for transfers between devices, along_chips(): lax.ppermute(value, 'out', [(r, (r + PAIR) % out_count) for r in range(ou...  9.8 us
    ppermute x5, starting transfers between devices, along_chips(): lax.ppermute(value, 'out', [(r, (r + PAIR) % out_count) for r in range(ou...  7.91 us
    ppermute x4, starting transfers between devices, across_sides(): return lax.ppermute(value, 'in', [(s, s ^ 1) for s in range(in_count)])  6.19 us
    unnamed x10, local copies, waits for them, and re-layouts  4.28 us
  transfers between devices with their start and end apart: 25, of which 13 were waited for; matrix products, arithmetic and copies ran while one was open for 0% of the time, Pallas kernels for 12%

commit v1 on v0

--- a/solution.py
+++ b/solution.py
@@ -11,7 +11,8 @@
 PAIR = 2
 TOP = 32767.0
 GROUPS = 4
-WEIGHTS = (4000, 50000)
+KERNEL_WEIGHT = 1
+SUMS_WEIGHT = 1
 KERNEL_MEMORY = 24 << 20
 LANES = 128
 
@@ -77,7 +78,7 @@
     return pltpu.with_memory_space_constraint(value, pltpu.VMEM)
 
 
-def kernel_call(kernel, name, inputs, in_table, outputs, scratch, flops, transcendentals):
+def kernel_call(kernel, name, inputs, in_table, outputs, scratch, flops, transcendentals, weight=KERNEL_WEIGHT):
     moved = sum(math.prod(array.shape) * jnp.dtype(array.dtype).itemsize for array in [*inputs, *outputs])
     memory = pl.BlockSpec(memory_space=pltpu.VMEM)
     return pl.pallas_call(
@@ -88,7 +89,7 @@
         out_specs=[memory] * len(outputs),
         scratch_shapes=scratch,
         compiler_params=pltpu.CompilerParams(vmem_limit_bytes=KERNEL_MEMORY),
-        cost_estimate=pl.CostEstimate(flops=4 * flops, bytes_accessed=4 * moved, transcendentals=transcendentals),
+        cost_estimate=pl.CostEstimate(flops=weight * flops, bytes_accessed=weight * moved, transcendentals=transcendentals),
     )(*inputs)
 
 
@@ -186,22 +187,6 @@
     ]
 
 
-def decode_kernel(coded, result):
-    total = result.shape[0]
-    for group, parts in enumerate(row_ranges(total)):
-        for part, (rows, unpack) in enumerate(zip(parts, (unpack_high, unpack_low))):
-            place = total // PAIR + part * GROUPS + group
-            result[rows, :] = unpack(coded[parts[0], :], coded[place:place + 1, :])
-
-
-def decoded_sums(coded, rows, weight):
-    cells = coded.shape[1]
-    return kernel_call(
-        decode_kernel, "decoded_sums", [coded], 0, [pltpu.VMEM((rows, cells), jnp.float32)], [],
-        weight * rows * cells, 0,
-    )[0]
-
-
 def sums_kernel(arrivals, table, kept, received, *refs):
     arrived, pieces, result = refs[:arrivals], refs[arrivals:-1], refs[-1]
     total = kept.shape[1]
@@ -212,7 +197,7 @@
             value = blocks_times_products(wanted, kept, received, pieces, rows)
             place = total // PAIR + part * GROUPS + group
             for ref in arrived:
-                value = value + ref[rows, :]
+                value = value + unpack(ref[parts[0], :], ref[place:place + 1, :])
             if result.dtype == jnp.int32:
                 code, exponent = encode(value)
                 codes.append(code)
@@ -227,7 +212,7 @@
     terms, rows, cells = kept.shape
     return kernel_call(
         functools.partial(sums_kernel, len(arrived)), name, [table, kept, received, *arrived, *pieces], 1,
-        [result], [], 8 * terms * rows * cells, rows * cells,
+        [result], [], 8 * terms * rows * cells, rows * cells, SUMS_WEIGHT,
     )[0]
 
 
@@ -278,20 +263,17 @@
         sent.append(products[1])
         received.append(near(across_sides(after(products[1], *received[-1:]))))
     core_own = across_cores(diff_blocks)
-
-    arrived, ahead = [], sent
-    for step in range(columns):
-        last = step == columns - 1
-        waits = [far_field] if step == 0 else rings[columns - 2:columns - 1] if last else []
-        far = along_chips(after(rings[step], *waits))
-        pieces = [own_blocks if last else near(rings[step]), near(far)]
-        pieces += [near(core_own if last else across_cores(after(rings[step], *ahead))), near(across_cores(after(far, *ahead)))]
-        if last:
-            return final_sums(block_table, kept[step], received[step], arrived, pieces)
+    arrived = []
+    for step in range(columns - 1):
+        far = along_chips(after(rings[step], far_field))
+        ahead = [total, *rings[step + 1:columns - 1]] if step > 0 else [*sent, core_own]
+        pieces = [near(rings[step]), near(far), near(across_cores(after(rings[step], *ahead)))]
+        pieces.append(near(across_cores(after(far, *([*arrived, received[step]] if step > 0 else sent)))))
         total = partial_sums(block_table, kept[step], received[step], arrived, pieces)
-        coming = near(along_columns(total, -1))
-        arrived = [decoded_sums(coming, kernel_weights.shape[1], WEIGHTS[step == columns - 2])]
-        ahead = [total, *([core_own] if step == 0 else [])]
+        arrived = [near(along_columns(total, -1))]
+    far_own = along_chips(after(diff_blocks, rings[columns - 2]))
+    pieces = [own_blocks, near(far_own), near(core_own), near(across_cores(after(far_own, *arrived, received[-1])))]
+    return final_sums(block_table, kept[-1], received[-1], arrived, pieces)
 
 
 def solution(mesh):

time: 93.1 us -> 88.4 us (0.950)
  starting transfers between devices: 35.3 us -> 28.8 us
  waiting for transfers between devices: 39.7 us -> 41.8 us
    ppermute x5, waiting for transfers between devices: 9.8 us -> 19.8 us  [along_chips(): lax.ppermute(value, 'out', [(r, (r + PAIR) % out_count) for r in range(ou...]
    ppermute x6, starting transfers between devices: 20.5 us -> 14.5 us  [along_columns(): lax.ppermute(value, 'in', [(s, (s + PAIR * shift) % in_count) for s in ra...]
    ppermute x6, waiting for transfers between devices: 19.7 us -> 14.7 us  [along_columns(): lax.ppermute(value, 'in', [(s, (s + PAIR * shift) % in_count) for s in ra...]
    ppermute x4, waiting for transfers between devices: 10.1 us -> 5.34 us  [across_sides(): return lax.ppermute(value, 'in', [(s, s ^ 1) for s in range(in_count)])]
    ppermute x10, waiting for transfers between devices: 0.03 us -> 1.93 us  [across_cores(): return lax.ppermute(value, 'out', [(r, r ^ 1) for r in range(out_count)])]
    pallas_call x12 -> x9, Pallas kernels: 13.3 us -> 13.2 us  [kernel_call(): pl.pallas_call(kernel, name=name, out_shape=outputs, in_specs=[pl.BlockSp...]
  transfers between devices with their start and end apart: 25 -> 25, of which waited for: 13 -> 8; matrix products, arithmetic and copies ran while one was open for 0% -> 0% of each run, Pallas kernels for 12% -> 13%
where the time goes in v1:
time: 88.4 us; the launch traced here: 88.2 us
  waiting for transfers between devices  41.8 us (47%)
  starting transfers between devices  28.8 us (33%)
  Pallas kernels  13.2 us (15%)
  local copies, waits for them, and re-layouts  4.28 us (5%)
    ppermute x5, waiting for transfers between devices, along_chips(): lax.ppermute(value, 'out', [(r, (r + PAIR) % out_count) for r in range(ou...  19.8 us
    ppermute x6, waiting for transfers between devices, along_columns(): lax.ppermute(value, 'in', [(s, (s + PAIR * shift) % in_count) for s in ra...  14.7 us
    ppermute x6, starting transfers between devices, along_columns(): lax.ppermute(value, 'in', [(s, (s + PAIR * shift) % in_count) for s in ra...  14.5 us
    pallas_call x9, Pallas kernels, kernel_call(): pl.pallas_call(kernel, name=name, out_shape=outputs, in_specs=[pl.BlockSp...  13.2 us
    ppermute x5, starting transfers between devices, along_chips(): lax.ppermute(value, 'out', [(r, (r + PAIR) % out_count) for r in range(ou...  7.9 us
    ppermute x4, waiting for transfers between devices, across_sides(): return lax.ppermute(value, 'in', [(s, s ^ 1) for s in range(in_count)])  5.34 us
    ppermute x4, starting transfers between devices, across_sides(): return lax.ppermute(value, 'in', [(s, s ^ 1) for s in range(in_count)])  5.3 us
    unnamed x10, local copies, waits for them, and re-layouts  4.28 us
  transfers between devices with their start and end apart: 25, of which 8 were waited for; matrix products, arithmetic and copies ran while one was open for 0% of the time, Pallas kernels for 13%

profile of v1, /device:TPU:0, one launch (start us, length us, event | category | flops | bytes accessed | tf_op | source)
XLA Modules:
  0.0 88.2 jit_solution(9016638764932232356)
XLA Ops:
  0.0 2.9 %collective-permute-start = (bf16[1024,256]{1,0:T(8,128)(2,1)}, bf16[1024,256]{1,0:T(8,128)(2,1)S(1)}, u32[]{:S(2)}, u32[]{:S(2)}) collective-permute-start(bf16[1024,256]{1,0:T(8,128)(2,1)} %refs_1_.1), channel_id=1, source_target_pairs={{0,16},{8,24},{16,0},{24,8},{1,17},{9,25},{17,1},{25,9},{2,18},{10... | collective-permute-start | bytes 1572872 | tf_op jit(solution)/shard_map/ppermute | solution.py:242
  2.9 3.6 %collective-permute-start.2 = (bf16[2,1024,128]{2,1,0:T(8,128)(2,1)}, bf16[2,1024,128]{2,1,0:T(8,128)(2,1)S(1)}, u32[]{:S(2)}, u32[]{:S(2)}) collective-permute-start(bf16[2,1024,128]{2,1,0:T(8,128)(2,1)} %refs_2_.1), channel_id=1, source_target_pairs={{0,6},{1,7},{2,0},{3,1},{4,2},{5,3},{6,4},{7,5},{8,14},{9,15},{10,... | collective-permute-start | bytes 1572872 | tf_op jit(solution)/shard_map/ppermute | solution.py:248
  6.5 2.2 %copy-done = bf16[2,1024,1024]{2,1,0:T(8,128)(2,1)S(1)} copy-done((bf16[2,1024,1024]{2,1,0:T(8,128)(2,1)S(1)}, bf16[2,1024,1024]{2,1,0:T(8,128)(2,1)}, u32[]{:S(2)}) %copy-start) | copy-done | bytes 4194328
  11.2 3.9 %collective-permute-done.refs_1_ = bf16[1024,256]{1,0:T(8,128)(2,1)S(1)} collective-permute-done((bf16[1024,256]{1,0:T(8,128)(2,1)}, bf16[1024,256]{1,0:T(8,128)(2,1)S(1)}, u32[]{:S(2)}, u32[]{:S(2)}) %collective-permute-start) | collective-permute-done | bytes 524320 | tf_op jit(solution)/shard_map/ppermute | solution.py:242
  15.6 2.2 %collective-permute-done.2.refs_0_ = bf16[2,1024,128]{2,1,0:T(8,128)(2,1)S(1)} collective-permute-done((bf16[2,1024,128]{2,1,0:T(8,128)(2,1)}, bf16[2,1024,128]{2,1,0:T(8,128)(2,1)S(1)}, u32[]{:S(2)}, u32[]{:S(2)}) %collective-permute-start.2) | collective-permute-done | bytes 524320 | tf_op jit(solution)/shard_map/ppermute | solution.py:248
  18.3 4.2 %collective-permute-start.13 = (bf16[2,1024,128]{2,1,0:T(8,128)(2,1)S(1)}, bf16[2,1024,128]{2,1,0:T(8,128)(2,1)S(1)}, u32[]{:S(2)}, u32[]{:S(2)}) collective-permute-start(bf16[2,1024,128]{2,1,0:T(8,128)(2,1)S(1)} %collective-permute-done.2.refs_0_), channel_id=1, source_target_pairs={{0,6},{1,7},{2,0},{3,1},{4,2},{5,3},{6,4},{7,5},{8,14},{9,15},{10,... | collective-permute-start | bytes 1572872 | tf_op jit(solution)/shard_map/ppermute | solution.py:248
  24.0 1.6 %collective-permute-start.4 = (s32[1032,128]{1,0:T(8,128)S(1)}, s32[1032,128]{1,0:T(8,128)S(1)}, u32[]{:S(2)}, u32[]{:S(2)}) collective-permute-start(s32[1032,128]{1,0:T(8,128)S(1)} %get-tuple-element.40), channel_id=1, source_target_pairs={{0,1},{1,0},{2,3},{3,2},{4,5},{5,4},{6,7},{7,6},{8,9},{9,8},{10,11... | collective-permute-start | bytes 1585160 | tf_op jit(solution)/shard_map/ppermute | solution.py:245
  25.6 1.5 %products.4 = (f32[2,1024,128]{2,1,0:T(8,128)S(1)}, s32[1032,128]{1,0:T(8,128)S(1)}) custom-call(bf16[2,1024,1024]{2,1,0:T(8,128)(2,1)S(1)} %get-tuple-element.32.weights, bf16[1024,256]{1,0:T(8,128)(2,1)S(1)} %get-tuple-element.33.refs_0_, bf16[1024,256]{1,0:T(8,128)(2,1)S(1)} %collective-permute-done.refs_1_, ...), custom_call_target="tpu_custom_call" | custom-call | flops 1073741824 | bytes 7868416 | tf_op jit(solution)/shard_map/products/pallas_call | solution.py:84
  27.1 1.6 %products.5 = (f32[2,1024,128]{2,1,0:T(8,128)S(1)}, s32[1032,128]{1,0:T(8,128)S(1)}) custom-call(bf16[2,1024,1024]{2,1,0:T(8,128)(2,1)S(1)} %get-tuple-element.32.weights, bf16[1024,256]{1,0:T(8,128)(2,1)S(1)} %get-tuple-element.33.refs_0_, bf16[1024,256]{1,0:T(8,128)(2,1)S(1)} %collective-permute-done.refs_1_, ...), custom_call_target="tpu_custom_call" | custom-call | flops 1073741824 | bytes 7868416 | tf_op jit(solution)/shard_map/products/pallas_call | solution.py:84
  28.7 1.6 %products.6 = (f32[2,1024,128]{2,1,0:T(8,128)S(1)}, s32[1032,128]{1,0:T(8,128)S(1)}) custom-call(bf16[2,1024,1024]{2,1,0:T(8,128)(2,1)S(1)} %get-tuple-element.32.weights, bf16[1024,256]{1,0:T(8,128)(2,1)S(1)} %get-tuple-element.33.refs_0_, bf16[1024,256]{1,0:T(8,128)(2,1)S(1)} %collective-permute-done.refs_1_, ...), custom_call_target="tpu_custom_call" | custom-call | flops 1073741824 | bytes 7868416 | tf_op jit(solution)/shard_map/products/pallas_call | solution.py:84
  30.9 5.3 %collective-permute-done.4.received = s32[1032,128]{1,0:T(8,128)S(1)} collective-permute-done((s32[1032,128]{1,0:T(8,128)S(1)}, s32[1032,128]{1,0:T(8,128)S(1)}, u32[]{:S(2)}, u32[]{:S(2)}) %collective-permute-start.4) | collective-permute-done | bytes 528416 | tf_op jit(solution)/shard_map/ppermute | solution.py:245
  36.2 1.6 %collective-permute-start.5 = (s32[1032,128]{1,0:T(8,128)S(1)}, s32[1032,128]{1,0:T(8,128)S(1)}, u32[]{:S(2)}, u32[]{:S(2)}) collective-permute-start(s32[1032,128]{1,0:T(8,128)S(1)} %get-tuple-element.41), channel_id=1, source_target_pairs={{0,1},{1,0},{2,3},{3,2},{4,5},{5,4},{6,7},{7,6},{8,9},{9,8},{10,11... | collective-permute-start | bytes 1585160 | tf_op jit(solution)/shard_map/ppermute | solution.py:245
  39.5 1.5 %partial_sums.3 = s32[520,128]{1,0:T(8,128)S(1)} custom-call(s32[4,8]{1,0:T(4,128)S(1)} %copy-done.4, f32[2,1024,128]{2,1,0:T(8,128)S(1)} %get-tuple-element.46.kept, s32[1032,128]{1,0:T(8,128)S(1)} %collective-permute-done.4.received, bf16[2,1024,128]{2,1,0:T(8,128)(2,1)S(1)} %collective-permute-done.2.refs_0_, ...), custom_call_target="tpu_custom_call" | custom-call | flops 2097152 | bytes 3940480 | tf_op jit(solution)/shard_map/partial_sums/pallas_call | solution.py:84
  41.6 9.7 %collective-permute-done.15.refs_1_ = bf16[2,1024,128]{2,1,0:T(8,128)(2,1)S(1)} collective-permute-done((bf16[2,1024,128]{2,1,0:T(8,128)(2,1)S(1)}, bf16[2,1024,128]{2,1,0:T(8,128)(2,1)S(1)}, u32[]{:S(2)}, u32[]{:S(2)}) %collective-permute-start.15) | collective-permute-done | bytes 524320 | tf_op jit(solution)/shard_map/ppermute | solution.py:248
  51.2 2.8 %collective-permute-done.12.refs_0_ = s32[520,128]{1,0:T(8,128)S(1)} collective-permute-done((s32[520,128]{1,0:T(8,128)S(1)}, s32[520,128]{1,0:T(8,128)S(1)}, u32[]{:S(2)}, u32[]{:S(2)}) %collective-permute-start.12) | collective-permute-done | bytes 266272 | tf_op jit(solution)/shard_map/ppermute | solution.py:248
  56.0 1.6 %partial_sums.4 = s32[520,128]{1,0:T(8,128)S(1)} custom-call(s32[4,8]{1,0:T(4,128)S(1)} %copy-done.4, f32[2,1024,128]{2,1,0:T(8,128)S(1)} %get-tuple-element.45.kept, s32[1032,128]{1,0:T(8,128)S(1)} %collective-permute-done.5.received, s32[520,128]{1,0:T(8,128)S(1)} %collective-permute-done.12.refs_0_, ...), custom_call_target="tpu_custom_call" | custom-call | flops 2097152 | bytes 4206720 | tf_op jit(solution)/shard_map/partial_sums/pallas_call | solution.py:84
  57.6 3.4 %collective-permute-start.18 = (s32[520,128]{1,0:T(8,128)S(1)}, s32[520,128]{1,0:T(8,128)S(1)}, u32[]{:S(2)}, u32[]{:S(2)}) collective-permute-start(s32[520,128]{1,0:T(8,128)S(1)} %partial_sums.4), channel_id=1, source_target_pairs={{0,6},{1,7},{2,0},{3,1},{4,2},{5,3},{6,4},{7,5},{8,14},{9,15},{10,... | collective-permute-start | bytes 798728 | tf_op jit(solution)/shard_map/ppermute | solution.py:248
  61.1 7.5 %collective-permute-done.19.refs_2_ = bf16[2,1024,128]{2,1,0:T(8,128)(2,1)S(1)} collective-permute-done((bf16[2,1024,128]{2,1,0:T(8,128)(2,1)S(1)}, bf16[2,1024,128]{2,1,0:T(8,128)(2,1)S(1)}, u32[]{:S(2)}, u32[]{:S(2)}) %collective-permute-start.19) | collective-permute-done | bytes 524320 | tf_op jit(solution)/shard_map/ppermute | solution.py:242
  68.6 1.6 %collective-permute-start.7 = (s32[1032,128]{1,0:T(8,128)S(1)}, s32[1032,128]{1,0:T(8,128)S(1)}, u32[]{:S(2)}, u32[]{:S(2)}) collective-permute-start(s32[1032,128]{1,0:T(8,128)S(1)} %get-tuple-element.43), channel_id=1, source_target_pairs={{0,1},{1,0},{2,3},{3,2},{4,5},{5,4},{6,7},{7,6},{8,9},{9,8},{10,11... | collective-permute-start | bytes 1585160 | tf_op jit(solution)/shard_map/ppermute | solution.py:245
  71.7 1.6 %partial_sums.5 = s32[520,128]{1,0:T(8,128)S(1)} custom-call(s32[4,8]{1,0:T(4,128)S(1)} %copy-done.4, f32[2,1024,128]{2,1,0:T(8,128)S(1)} %get-tuple-element.44.kept, s32[1032,128]{1,0:T(8,128)S(1)} %collective-permute-done.6.received, s32[520,128]{1,0:T(8,128)S(1)} %collective-permute-done.18.refs_0_, ...), custom_call_target="tpu_custom_call" | custom-call | flops 2097152 | bytes 4206720 | tf_op jit(solution)/shard_map/partial_sums/pallas_call | solution.py:84
  73.3 2.6 %collective-permute-start.22 = (s32[520,128]{1,0:T(8,128)S(1)}, s32[520,128]{1,0:T(8,128)S(1)}, u32[]{:S(2)}, u32[]{:S(2)}) collective-permute-start(s32[520,128]{1,0:T(8,128)S(1)} %partial_sums.5), channel_id=1, source_target_pairs={{0,6},{1,7},{2,0},{3,1},{4,2},{5,3},{6,4},{7,5},{8,14},{9,15},{10,... | collective-permute-start | bytes 798728 | tf_op jit(solution)/shard_map/ppermute | solution.py:248
  75.9 8.3 %collective-permute-done.23.refs_2_ = bf16[2,1024,128]{2,1,0:T(8,128)(2,1)S(1)} collective-permute-done((bf16[2,1024,128]{2,1,0:T(8,128)(2,1)S(1)}, bf16[2,1024,128]{2,1,0:T(8,128)(2,1)S(1)}, u32[]{:S(2)}, u32[]{:S(2)}) %collective-permute-start.23) | collective-permute-done | bytes 524320 | tf_op jit(solution)/shard_map/ppermute | solution.py:242
  84.3 1.9 %collective-permute-done.24.refs_4_ = bf16[2,1024,128]{2,1,0:T(8,128)(2,1)S(1)} collective-permute-done((bf16[2,1024,128]{2,1,0:T(8,128)(2,1)S(1)}, bf16[2,1024,128]{2,1,0:T(8,128)(2,1)S(1)}, u32[]{:S(2)}, u32[]{:S(2)}) %collective-permute-start.24) | collective-permute-done | bytes 524320 | tf_op jit(solution)/shard_map/ppermute | solution.py:239
  86.2 2.0 %final_sums.1 = bf16[1024,128]{1,0:T(8,128)(2,1)} custom-call(s32[4,8]{1,0:T(4,128)S(1)} %copy-done.4, f32[2,1024,128]{2,1,0:T(8,128)S(1)} %get-tuple-element.36.kept, s32[1032,128]{1,0:T(8,128)S(1)} %collective-permute-done.7.received, s32[520,128]{1,0:T(8,128)S(1)} %collective-permute-done.22.refs_0_, bf16[2,1024,128]{2,1,0:T(8,128)(2,1)S(1)} %get-tuple-element.56.refs_1_, ...), custom_call_target="tpu_custom_call" | custom-call | flops 2097152 | bytes 4202624 | tf_op jit(solution)/shard_map/final_sums/pallas_call | solution.py:84
  (45 shorter events, 11.2 us)
Async XLA Ops:
  0.0 15.1 %collective-permute-start = (bf16[1024,256]{1,0:T(8,128)(2,1)}, bf16[1024,256]{1,0:T(8,128)(2,1)S(1)}, u32[]{:S(2)}, u32[]{:S(2)}) collective-permute-start(bf16[1024,256]{1,0:T(8,128)(2,1)} %refs_1_.1), channel_id=1, source_target_pairs={{0,16},{8,24},{16,0},{24,8},{1,17},{9,25},{17,1},{25,9},{2,18},{10... | collective-permute-start | bytes 1572872 | tf_op jit(solution)/shard_map/ppermute | solution.py:242
  2.9 14.8 %collective-permute-start.2 = (bf16[2,1024,128]{2,1,0:T(8,128)(2,1)}, bf16[2,1024,128]{2,1,0:T(8,128)(2,1)S(1)}, u32[]{:S(2)}, u32[]{:S(2)}) collective-permute-start(bf16[2,1024,128]{2,1,0:T(8,128)(2,1)} %refs_2_.1), channel_id=1, source_target_pairs={{0,6},{1,7},{2,0},{3,1},{4,2},{5,3},{6,4},{7,5},{8,14},{9,15},{10,... | collective-permute-start | bytes 1572872 | tf_op jit(solution)/shard_map/ppermute | solution.py:248
  6.5 11.8 %collective-permute-start.1 = (bf16[1024,256]{1,0:T(8,128)(2,1)}, bf16[1024,256]{1,0:T(8,128)(2,1)S(1)}, u32[]{:S(2)}, u32[]{:S(2)}) collective-permute-start(bf16[1024,256]{1,0:T(8,128)(2,1)} %refs_1_.1), channel_id=1, source_target_pairs={{0,8},{8,0},{16,24},{24,16},{1,9},{9,1},{17,25},{25,17},{2,10},{10... | collective-permute-start | bytes 1572872 | tf_op jit(solution)/shard_map/ppermute | solution.py:239
  15.1 7.4 %collective-permute-start.3 = (bf16[1024,256]{1,0:T(8,128)(2,1)S(1)}, bf16[1024,256]{1,0:T(8,128)(2,1)S(1)}, u32[]{:S(2)}, u32[]{:S(2)}) collective-permute-start(bf16[1024,256]{1,0:T(8,128)(2,1)S(1)} %collective-permute-done.refs_1_), channel_id=1, source_target_pairs={{0,8},{8,0},{16,24},{24,16},{1,9},{9,1},{17,25},{25,17},{2,10},{10... | collective-permute-start | bytes 1572872 | tf_op jit(solution)/shard_map/ppermute | solution.py:239
  15.1 15.2 %collective-permute-start.9 = (bf16[2,1024,128]{2,1,0:T(8,128)(2,1)S(1)}, bf16[2,1024,128]{2,1,0:T(8,128)(2,1)S(1)}, u32[]{:S(2)}, u32[]{:S(2)}) collective-permute-start(bf16[2,1024,128]{2,1,0:T(8,128)(2,1)S(1)} %copy-done.2), channel_id=1, source_target_pairs={{0,8},{8,0},{16,24},{24,16},{1,9},{9,1},{17,25},{25,17},{2,10},{10... | collective-permute-start | bytes 1572872 | tf_op jit(solution)/shard_map/ppermute | solution.py:239
  17.8 12.6 %collective-permute-start.8 = (bf16[2,1024,128]{2,1,0:T(8,128)(2,1)S(1)}, bf16[2,1024,128]{2,1,0:T(8,128)(2,1)S(1)}, u32[]{:S(2)}, u32[]{:S(2)}) collective-permute-start(bf16[2,1024,128]{2,1,0:T(8,128)(2,1)S(1)} %collective-permute-done.2.refs_0_), channel_id=1, source_target_pairs={{0,16},{8,24},{16,0},{24,8},{1,17},{9,25},{17,1},{25,9},{2,18},{10... | collective-permute-start | bytes 1572872 | tf_op jit(solution)/shard_map/ppermute | solution.py:242
  18.3 19.5 %collective-permute-start.13 = (bf16[2,1024,128]{2,1,0:T(8,128)(2,1)S(1)}, bf16[2,1024,128]{2,1,0:T(8,128)(2,1)S(1)}, u32[]{:S(2)}, u32[]{:S(2)}) collective-permute-start(bf16[2,1024,128]{2,1,0:T(8,128)(2,1)S(1)} %collective-permute-done.2.refs_0_), channel_id=1, source_target_pairs={{0,6},{1,7},{2,0},{3,1},{4,2},{5,3},{6,4},{7,5},{8,14},{9,15},{10,... | collective-permute-start | bytes 1572872 | tf_op jit(solution)/shard_map/ppermute | solution.py:248
  24.0 12.2 %collective-permute-start.4 = (s32[1032,128]{1,0:T(8,128)S(1)}, s32[1032,128]{1,0:T(8,128)S(1)}, u32[]{:S(2)}, u32[]{:S(2)}) collective-permute-start(s32[1032,128]{1,0:T(8,128)S(1)} %get-tuple-element.40), channel_id=1, source_target_pairs={{0,1},{1,0},{2,3},{3,2},{4,5},{5,4},{6,7},{7,6},{8,9},{9,8},{10,11... | collective-permute-start | bytes 1585160 | tf_op jit(solution)/shard_map/ppermute | solution.py:245
  30.3 9.2 %collective-permute-start.10 = (bf16[2,1024,128]{2,1,0:T(8,128)(2,1)S(1)}, bf16[2,1024,128]{2,1,0:T(8,128)(2,1)S(1)}, u32[]{:S(2)}, u32[]{:S(2)}) collective-permute-start(bf16[2,1024,128]{2,1,0:T(8,128)(2,1)S(1)} %collective-permute-done.2.refs_0_), channel_id=1, source_target_pairs={{0,8},{8,0},{16,24},{24,16},{1,9},{9,1},{17,25},{25,17},{2,10},{10... | collective-permute-start | bytes 1572872 | tf_op jit(solution)/shard_map/ppermute | solution.py:239
  30.4 9.1 %collective-permute-start.11 = (bf16[2,1024,128]{2,1,0:T(8,128)(2,1)S(1)}, bf16[2,1024,128]{2,1,0:T(8,128)(2,1)S(1)}, u32[]{:S(2)}, u32[]{:S(2)}) collective-permute-start(bf16[2,1024,128]{2,1,0:T(8,128)(2,1)S(1)} %collective-permute-done.8.refs_1_), channel_id=1, source_target_pairs={{0,8},{8,0},{16,24},{24,16},{1,9},{9,1},{17,25},{25,17},{2,10},{10... | collective-permute-start | bytes 1572872 | tf_op jit(solution)/shard_map/ppermute | solution.py:239
  36.2 17.9 %collective-permute-start.5 = (s32[1032,128]{1,0:T(8,128)S(1)}, s32[1032,128]{1,0:T(8,128)S(1)}, u32[]{:S(2)}, u32[]{:S(2)}) collective-permute-start(s32[1032,128]{1,0:T(8,128)S(1)} %get-tuple-element.41), channel_id=1, source_target_pairs={{0,1},{1,0},{2,3},{3,2},{4,5},{5,4},{6,7},{7,6},{8,9},{9,8},{10,11... | collective-permute-start | bytes 1585160 | tf_op jit(solution)/shard_map/ppermute | solution.py:245
  37.8 13.4 %collective-permute-start.15 = (bf16[2,1024,128]{2,1,0:T(8,128)(2,1)S(1)}, bf16[2,1024,128]{2,1,0:T(8,128)(2,1)S(1)}, u32[]{:S(2)}, u32[]{:S(2)}) collective-permute-start(bf16[2,1024,128]{2,1,0:T(8,128)(2,1)S(1)} %collective-permute-done.13.refs_1_), channel_id=1, source_target_pairs={{0,6},{1,7},{2,0},{3,1},{4,2},{5,3},{6,4},{7,5},{8,14},{9,15},{10,... | collective-permute-start | bytes 1572872 | tf_op jit(solution)/shard_map/ppermute | solution.py:248
  38.0 13.2 %collective-permute-start.14 = (bf16[2,1024,128]{2,1,0:T(8,128)(2,1)S(1)}, bf16[2,1024,128]{2,1,0:T(8,128)(2,1)S(1)}, u32[]{:S(2)}, u32[]{:S(2)}) collective-permute-start(bf16[2,1024,128]{2,1,0:T(8,128)(2,1)S(1)} %collective-permute-done.13.refs_1_), channel_id=1, source_target_pairs={{0,16},{8,24},{16,0},{24,8},{1,17},{9,25},{17,1},{25,9},{2,18},{10... | collective-permute-start | bytes 1572872 | tf_op jit(solution)/shard_map/ppermute | solution.py:242
  41.0 13.0 %collective-permute-start.12 = (s32[520,128]{1,0:T(8,128)S(1)}, s32[520,128]{1,0:T(8,128)S(1)}, u32[]{:S(2)}, u32[]{:S(2)}) collective-permute-start(s32[520,128]{1,0:T(8,128)S(1)} %partial_sums.3), channel_id=1, source_target_pairs={{0,6},{1,7},{2,0},{3,1},{4,2},{5,3},{6,4},{7,5},{8,14},{9,15},{10,... | collective-permute-start | bytes 798728 | tf_op jit(solution)/shard_map/ppermute | solution.py:248
  51.2 4.8 %collective-permute-start.16 = (bf16[2,1024,128]{2,1,0:T(8,128)(2,1)S(1)}, bf16[2,1024,128]{2,1,0:T(8,128)(2,1)S(1)}, u32[]{:S(2)}, u32[]{:S(2)}) collective-permute-start(bf16[2,1024,128]{2,1,0:T(8,128)(2,1)S(1)} %collective-permute-done.13.refs_1_), channel_id=1, source_target_pairs={{0,8},{8,0},{16,24},{24,16},{1,9},{9,1},{17,25},{25,17},{2,10},{10... | collective-permute-start | bytes 1572872 | tf_op jit(solution)/shard_map/ppermute | solution.py:239
  54.1 1.9 %collective-permute-start.17 = (bf16[2,1024,128]{2,1,0:T(8,128)(2,1)S(1)}, bf16[2,1024,128]{2,1,0:T(8,128)(2,1)S(1)}, u32[]{:S(2)}, u32[]{:S(2)}) collective-permute-start(bf16[2,1024,128]{2,1,0:T(8,128)(2,1)S(1)} %collective-permute-done.14.refs_2_), channel_id=1, source_target_pairs={{0,8},{8,0},{16,24},{24,16},{1,9},{9,1},{17,25},{25,17},{2,10},{10... | collective-permute-start | bytes 1572872 | tf_op jit(solution)/shard_map/ppermute | solution.py:239
  54.1 14.5 %collective-permute-start.6 = (s32[1032,128]{1,0:T(8,128)S(1)}, s32[1032,128]{1,0:T(8,128)S(1)}, u32[]{:S(2)}, u32[]{:S(2)}) collective-permute-start(s32[1032,128]{1,0:T(8,128)S(1)} %get-tuple-element.42), channel_id=1, source_target_pairs={{0,1},{1,0},{2,3},{3,2},{4,5},{5,4},{6,7},{7,6},{8,9},{9,8},{10,11... | collective-permute-start | bytes 1585160 | tf_op jit(solution)/shard_map/ppermute | solution.py:245
  54.5 14.1 %collective-permute-start.19 = (bf16[2,1024,128]{2,1,0:T(8,128)(2,1)S(1)}, bf16[2,1024,128]{2,1,0:T(8,128)(2,1)S(1)}, u32[]{:S(2)}, u32[]{:S(2)}) collective-permute-start(bf16[2,1024,128]{2,1,0:T(8,128)(2,1)S(1)} %collective-permute-done.15.refs_1_), channel_id=1, source_target_pairs={{0,16},{8,24},{16,0},{24,8},{1,17},{9,25},{17,1},{25,9},{2,18},{10... | collective-permute-start | bytes 1572872 | tf_op jit(solution)/shard_map/ppermute | solution.py:242
  57.6 11.0 %collective-permute-start.18 = (s32[520,128]{1,0:T(8,128)S(1)}, s32[520,128]{1,0:T(8,128)S(1)}, u32[]{:S(2)}, u32[]{:S(2)}) collective-permute-start(s32[520,128]{1,0:T(8,128)S(1)} %partial_sums.4), channel_id=1, source_target_pairs={{0,6},{1,7},{2,0},{3,1},{4,2},{5,3},{6,4},{7,5},{8,14},{9,15},{10,... | collective-permute-start | bytes 798728 | tf_op jit(solution)/shard_map/ppermute | solution.py:248
  61.1 10.7 %collective-permute-start.20 = (bf16[2,1024,128]{2,1,0:T(8,128)(2,1)S(1)}, bf16[2,1024,128]{2,1,0:T(8,128)(2,1)S(1)}, u32[]{:S(2)}, u32[]{:S(2)}) collective-permute-start(bf16[2,1024,128]{2,1,0:T(8,128)(2,1)S(1)} %collective-permute-done.15.refs_1_), channel_id=1, source_target_pairs={{0,8},{8,0},{16,24},{24,16},{1,9},{9,1},{17,25},{25,17},{2,10},{10... | collective-permute-start | bytes 1572872 | tf_op jit(solution)/shard_map/ppermute | solution.py:239
  68.6 3.1 %collective-permute-start.21 = (bf16[2,1024,128]{2,1,0:T(8,128)(2,1)S(1)}, bf16[2,1024,128]{2,1,0:T(8,128)(2,1)S(1)}, u32[]{:S(2)}, u32[]{:S(2)}) collective-permute-start(bf16[2,1024,128]{2,1,0:T(8,128)(2,1)S(1)} %collective-permute-done.19.refs_2_), channel_id=1, source_target_pairs={{0,8},{8,0},{16,24},{24,16},{1,9},{9,1},{17,25},{25,17},{2,10},{10... | collective-permute-start | bytes 1572872 | tf_op jit(solution)/shard_map/ppermute | solution.py:239
  68.6 15.6 %collective-permute-start.7 = (s32[1032,128]{1,0:T(8,128)S(1)}, s32[1032,128]{1,0:T(8,128)S(1)}, u32[]{:S(2)}, u32[]{:S(2)}) collective-permute-start(s32[1032,128]{1,0:T(8,128)S(1)} %get-tuple-element.43), channel_id=1, source_target_pairs={{0,1},{1,0},{2,3},{3,2},{4,5},{5,4},{6,7},{7,6},{8,9},{9,8},{10,11... | collective-permute-start | bytes 1585160 | tf_op jit(solution)/shard_map/ppermute | solution.py:245
  70.3 14.0 %collective-permute-start.23 = (bf16[2,1024,128]{2,1,0:T(8,128)(2,1)S(1)}, bf16[2,1024,128]{2,1,0:T(8,128)(2,1)S(1)}, u32[]{:S(2)}, u32[]{:S(2)}) collective-permute-start(bf16[2,1024,128]{2,1,0:T(8,128)(2,1)S(1)} %copy-done.3), channel_id=1, source_target_pairs={{0,16},{8,24},{16,0},{24,8},{1,17},{9,25},{17,1},{25,9},{2,18},{10... | collective-permute-start | bytes 1572872 | tf_op jit(solution)/shard_map/ppermute | solution.py:242
  73.3 10.9 %collective-permute-start.22 = (s32[520,128]{1,0:T(8,128)S(1)}, s32[520,128]{1,0:T(8,128)S(1)}, u32[]{:S(2)}, u32[]{:S(2)}) collective-permute-start(s32[520,128]{1,0:T(8,128)S(1)} %partial_sums.5), channel_id=1, source_target_pairs={{0,6},{1,7},{2,0},{3,1},{4,2},{5,3},{6,4},{7,5},{8,14},{9,15},{10,... | collective-permute-start | bytes 798728 | tf_op jit(solution)/shard_map/ppermute | solution.py:248
  (6 other events, 57.0 us)

commit v2 on v1

--- a/solution.py
+++ b/solution.py
@@ -11,8 +11,7 @@
 PAIR = 2
 TOP = 32767.0
 GROUPS = 4
-KERNEL_WEIGHT = 1
-SUMS_WEIGHT = 1
+UNPACK_COST = 30000
 KERNEL_MEMORY = 24 << 20
 LANES = 128
 
@@ -78,7 +77,7 @@
     return pltpu.with_memory_space_constraint(value, pltpu.VMEM)
 
 
-def kernel_call(kernel, name, inputs, in_table, outputs, scratch, flops, transcendentals, weight=KERNEL_WEIGHT):
+def kernel_call(kernel, name, inputs, in_table, outputs, scratch, flops, transcendentals):
     moved = sum(math.prod(array.shape) * jnp.dtype(array.dtype).itemsize for array in [*inputs, *outputs])
     memory = pl.BlockSpec(memory_space=pltpu.VMEM)
     return pl.pallas_call(
@@ -89,7 +88,7 @@
         out_specs=[memory] * len(outputs),
         scratch_shapes=scratch,
         compiler_params=pltpu.CompilerParams(vmem_limit_bytes=KERNEL_MEMORY),
-        cost_estimate=pl.CostEstimate(flops=weight * flops, bytes_accessed=weight * moved, transcendentals=transcendentals),
+        cost_estimate=pl.CostEstimate(flops=flops, bytes_accessed=moved, transcendentals=transcendentals),
     )(*inputs)
 
 
@@ -112,7 +111,7 @@
     rows = total // GROUPS
     half = kept.shape[2]
     in_index = lax.axis_index("in")
-    target = (in_index // PAIR + shift) % columns
+    target = (in_index // PAIR - shift + columns) % columns
     source = position(target, lax.axis_index("out"), len(fields) // PAIR)
     side = in_index % PAIR
 
@@ -161,15 +160,34 @@
     return [position(table[out_index, column * PAIR + which], out_index, chips) for which in (side, 1 - side)]
 
 
-def blocks_times_products(wanted, kept, received, pieces, rows):
-    total = kept.shape[1]
+def unpacked_products(received, rows, total):
     packed = received[rows, :]
     scale = total + rows.start // (total // GROUPS)
+    scales = [received[place:place + 1, :] for place in (scale, scale + GROUPS)]
+    return [unpack_high(packed, scales[0]), unpack_low(packed, scales[1])]
+
+
+def unpack_kernel(received, result):
+    total = result.shape[1]
+    for parts in row_ranges(total):
+        for rows in parts:
+            for term, product in enumerate(unpacked_products(received, rows, total)):
+                result[term, rows] = product
+
+
+def unpacked(received, like):
+    return kernel_call(
+        unpack_kernel, "unpacked_products", [received], 0, [pltpu.VMEM(like.shape, like.dtype)], [],
+        UNPACK_COST * like.size, 0,
+    )[0]
+
+
+def blocks_times_products(wanted, kept, received, pieces, rows, total):
     mine = [kept[0, rows], kept[1, rows]]
-    other = []
-    for term, unpack in enumerate((unpack_high, unpack_low)):
-        place = scale + term * GROUPS
-        other.append(unpack(packed, received[place:place + 1, :]))
+    if received.dtype == kept.dtype:
+        other = [received[0, rows], received[1, rows]]
+    else:
+        other = unpacked_products(received, rows, total)
     value = None
     for index, products in zip(wanted, (mine, other)):
         for term, product in enumerate(products):
@@ -194,7 +212,7 @@
     for group, parts in enumerate(row_ranges(total)):
         codes = []
         for part, (rows, unpack) in enumerate(zip(parts, (unpack_high, unpack_low))):
-            value = blocks_times_products(wanted, kept, received, pieces, rows)
+            value = blocks_times_products(wanted, kept, received, pieces, rows, total)
             place = total // PAIR + part * GROUPS + group
             for ref in arrived:
                 value = value + unpack(ref[parts[0], :], ref[place:place + 1, :])
@@ -212,7 +230,7 @@
     terms, rows, cells = kept.shape
     return kernel_call(
         functools.partial(sums_kernel, len(arrived)), name, [table, kept, received, *arrived, *pieces], 1,
-        [result], [], 8 * terms * rows * cells, rows * cells, SUMS_WEIGHT,
+        [result], [], 8 * terms * rows * cells, rows * cells,
     )[0]
 
 
@@ -247,33 +265,45 @@
     def along_columns(value, shift):
         return lax.ppermute(value, "in", [(s, (s + PAIR * shift) % in_count) for s in range(in_count)])
 
+    order = list(range(1, columns)) + [0]
     weights, own_field, own_blocks = load([kernel_weights, mode_field, diff_blocks])
+    far_field = after(along_chips(mode_field), weights)
+    fields = [own_field] + [near(field) for field in (far_field, across_cores(mode_field), across_cores(far_field))]
+
     rings = [diff_blocks]
     for step in range(1, columns):
         rings.append(along_columns(rings[-1], -1))
-    rings = rings[1:] + rings[:1]
-    far_field = after(along_chips(mode_field), weights)
-    core_field = after(across_cores(mode_field), rings[0])
-    fields = [own_field] + [near(field) for field in (far_field, core_field, across_cores(far_field))]
-
-    kept, received, sent = [], [], []
-    for step in range(columns):
-        products = multiply((step + 1) % columns, columns, weights, fields)
-        kept.append(products[0])
-        sent.append(products[1])
-        received.append(near(across_sides(after(products[1], *received[-1:]))))
+    kept, sent = {}, {}
+    for step in order:
+        kept[step], sent[step] = multiply(-step, columns, weights, fields)
     core_own = across_cores(diff_blocks)
-    arrived = []
-    for step in range(columns - 1):
-        far = along_chips(after(rings[step], far_field))
-        ahead = [total, *rings[step + 1:columns - 1]] if step > 0 else [*sent, core_own]
-        pieces = [near(rings[step]), near(far), near(across_cores(after(rings[step], *ahead)))]
-        pieces.append(near(across_cores(after(far, *([*arrived, received[step]] if step > 0 else sent)))))
-        total = partial_sums(block_table, kept[step], received[step], arrived, pieces)
-        arrived = [near(along_columns(total, -1))]
-    far_own = along_chips(after(diff_blocks, rings[columns - 2]))
-    pieces = [own_blocks, near(far_own), near(core_own), near(across_cores(after(far_own, *arrived, received[-1])))]
-    return final_sums(block_table, kept[-1], received[-1], arrived, pieces)
+    far_own = along_chips(after(diff_blocks, far_field))
+    far = [far_own]
+    for place, step in enumerate(order[:-1]):
+        earlier = [[far_field], [*sent.values(), core_own, far[-1]]][place] if place < 2 else far[-1:]
+        far.append(along_chips(after(rings[step], *earlier)))
+
+    received, coming, partials, pieces = {}, [], [], {}
+
+    def send_sums(place):
+        step = order[place]
+        near_pieces = [rings[step], far[place + 1]]
+        earlier = partials[-1:] if place == columns - 2 else []
+        pieces[step] = [near(piece) for piece in near_pieces]
+        pieces[step] += [near(across_cores(after(piece, *earlier))) for piece in near_pieces]
+        partials.append(partial_sums(block_table, kept[step], received[step], coming[-1:], pieces[step]))
+        coming.append(near(along_columns(partials[-1], -1)))
+        return partials[-1]
+
+    for place, step in enumerate(order):
+        earlier = [received[order[place - 1]]] if place > 0 else []
+        if place > 1:
+            earlier.append(send_sums(place - 2))
+        received[step] = near(across_sides(after(sent[step], *earlier)))
+    send_sums(columns - 2)
+    pieces[0] = [own_blocks, near(far_own), near(core_own), near(across_cores(after(far_own, coming[-1])))]
+    others = near(unpacked(received[0], kept[0]))
+    return final_sums(block_table, kept[0], others, coming[-1:], pieces[0])
 
 
 def solution(mesh):

time: 88.4 us -> 86.6 us (0.980)
  waiting for transfers between devices: 41.8 us -> 29.5 us
  starting transfers between devices: 28.8 us -> 39.3 us
    ppermute x6, starting transfers between devices: 14.5 us -> 25 us  [along_columns(): lax.ppermute(value, 'in', [(s, (s + PAIR * shift) % in_count) for s in ra...]
    ppermute x5, waiting for transfers between devices: 19.8 us -> 11.4 us  [along_chips(): lax.ppermute(value, 'out', [(r, (r + PAIR) % out_count) for r in range(ou...]
    ppermute x4, waiting for transfers between devices: 5.34 us -> 1.38 us  [across_sides(): return lax.ppermute(value, 'in', [(s, s ^ 1) for s in range(in_count)])]
    ppermute x5, starting transfers between devices: 7.9 us -> 6.99 us  [along_chips(): lax.ppermute(value, 'out', [(r, (r + PAIR) % out_count) for r in range(ou...]
    ppermute x4, starting transfers between devices: 5.3 us -> 6.2 us  [across_sides(): return lax.ppermute(value, 'in', [(s, s ^ 1) for s in range(in_count)])]
    pallas_call x9 -> x10, Pallas kernels: 13.2 us -> 13.2 us  [kernel_call(): pl.pallas_call(kernel, name=name, out_shape=outputs, in_specs=[pl.BlockSp...]
  transfers between devices with their start and end apart: 25 -> 25, of which waited for: 8 -> 12; matrix products, arithmetic and copies ran while one was open for 0% -> 0% of each run, Pallas kernels for 13% -> 13%
where the time goes in v2:
time: 86.6 us; the launch traced here: 86.4 us
  starting transfers between devices  39.3 us (45%)
  waiting for transfers between devices  29.5 us (34%)
  Pallas kernels  13.2 us (15%)
  local copies, waits for them, and re-layouts  4.28 us (5%)
    ppermute x6, starting transfers between devices, along_columns(): lax.ppermute(value, 'in', [(s, (s + PAIR * shift) % in_count) for s in ra...  25 us
    ppermute x6, waiting for transfers between devices, along_columns(): lax.ppermute(value, 'in', [(s, (s + PAIR * shift) % in_count) for s in ra...  15 us
    pallas_call x10, Pallas kernels, kernel_call(): pl.pallas_call(kernel, name=name, out_shape=outputs, in_specs=[pl.BlockSp...  13.2 us
    ppermute x5, waiting for transfers between devices, along_chips(): lax.ppermute(value, 'out', [(r, (r + PAIR) % out_count) for r in range(ou...  11.4 us
    ppermute x5, starting transfers between devices, along_chips(): lax.ppermute(value, 'out', [(r, (r + PAIR) % out_count) for r in range(ou...  6.99 us
    ppermute x4, starting transfers between devices, across_sides(): return lax.ppermute(value, 'in', [(s, s ^ 1) for s in range(in_count)])  6.2 us
    unnamed x10, local copies, waits for them, and re-layouts  4.28 us
  transfers between devices with their start and end apart: 25, of which 12 were waited for; matrix products, arithmetic and copies ran while one was open for 0% of the time, Pallas kernels for 13%

profile of v2, /device:TPU:0, one launch (start us, length us, event | category | flops | bytes accessed | tf_op | source)
XLA Modules:
  0.0 86.4 jit_solution(13132174594414089429)
XLA Ops:
  0.0 2.9 %collective-permute-start = (bf16[1024,256]{1,0:T(8,128)(2,1)}, bf16[1024,256]{1,0:T(8,128)(2,1)S(1)}, u32[]{:S(2)}, u32[]{:S(2)}) collective-permute-start(bf16[1024,256]{1,0:T(8,128)(2,1)} %refs_1_.1), channel_id=1, source_target_pairs={{0,16},{8,24},{16,0},{24,8},{1,17},{9,25},{17,1},{25,9},{2,18},{10... | collective-permute-start | bytes 1572872 | tf_op jit(solution)/shard_map/ppermute | solution.py:260
  2.9 3.6 %collective-permute-start.5 = (bf16[2,1024,128]{2,1,0:T(8,128)(2,1)}, bf16[2,1024,128]{2,1,0:T(8,128)(2,1)S(1)}, u32[]{:S(2)}, u32[]{:S(2)}) collective-permute-start(bf16[2,1024,128]{2,1,0:T(8,128)(2,1)} %refs_2_.1), channel_id=1, source_target_pairs={{0,6},{1,7},{2,0},{3,1},{4,2},{5,3},{6,4},{7,5},{8,14},{9,15},{10,... | collective-permute-start | bytes 1572872 | tf_op jit(solution)/shard_map/ppermute | solution.py:266
  6.5 2.2 %copy-done = bf16[2,1024,1024]{2,1,0:T(8,128)(2,1)S(1)} copy-done((bf16[2,1024,1024]{2,1,0:T(8,128)(2,1)S(1)}, bf16[2,1024,1024]{2,1,0:T(8,128)(2,1)}, u32[]{:S(2)}) %copy-start) | copy-done | bytes 4194328
  11.2 3.9 %collective-permute-done.refs_1_ = bf16[1024,256]{1,0:T(8,128)(2,1)S(1)} collective-permute-done((bf16[1024,256]{1,0:T(8,128)(2,1)}, bf16[1024,256]{1,0:T(8,128)(2,1)S(1)}, u32[]{:S(2)}, u32[]{:S(2)}) %collective-permute-start) | collective-permute-done | bytes 524320 | tf_op jit(solution)/shard_map/ppermute | solution.py:260
  15.6 2.2 %collective-permute-done.5.refs_0_ = bf16[2,1024,128]{2,1,0:T(8,128)(2,1)S(1)} collective-permute-done((bf16[2,1024,128]{2,1,0:T(8,128)(2,1)}, bf16[2,1024,128]{2,1,0:T(8,128)(2,1)S(1)}, u32[]{:S(2)}, u32[]{:S(2)}) %collective-permute-start.5) | collective-permute-done | bytes 524320 | tf_op jit(solution)/shard_map/ppermute | solution.py:266
  18.3 4.2 %collective-permute-start.11 = (bf16[2,1024,128]{2,1,0:T(8,128)(2,1)S(1)}, bf16[2,1024,128]{2,1,0:T(8,128)(2,1)S(1)}, u32[]{:S(2)}, u32[]{:S(2)}) collective-permute-start(bf16[2,1024,128]{2,1,0:T(8,128)(2,1)S(1)} %collective-permute-done.5.refs_0_), channel_id=1, source_target_pairs={{0,6},{1,7},{2,0},{3,1},{4,2},{5,3},{6,4},{7,5},{8,14},{9,15},{10,... | collective-permute-start | bytes 1572872 | tf_op jit(solution)/shard_map/ppermute | solution.py:266
  24.0 1.6 %collective-permute-start.3 = (s32[1032,128]{1,0:T(8,128)S(1)}, s32[1032,128]{1,0:T(8,128)S(1)}, u32[]{:S(2)}, u32[]{:S(2)}) collective-permute-start(s32[1032,128]{1,0:T(8,128)S(1)} %get-tuple-element.34), channel_id=1, source_target_pairs={{0,1},{1,0},{2,3},{3,2},{4,5},{5,4},{6,7},{7,6},{8,9},{9,8},{10,11... | collective-permute-start | bytes 1585160 | tf_op jit(solution)/shard_map/ppermute | solution.py:263
  27.2 1.6 %products.5 = (f32[2,1024,128]{2,1,0:T(8,128)S(1)}, s32[1032,128]{1,0:T(8,128)S(1)}) custom-call(bf16[2,1024,1024]{2,1,0:T(8,128)(2,1)S(1)} %get-tuple-element.27.weights, bf16[1024,256]{1,0:T(8,128)(2,1)S(1)} %get-tuple-element.28.refs_0_, bf16[1024,256]{1,0:T(8,128)(2,1)S(1)} %collective-permute-done.refs_1_, ...), custom_call_target="tpu_custom_call" | custom-call | flops 1073741824 | bytes 7868416 | tf_op jit(solution)/shard_map/products/pallas_call | solution.py:83
  28.7 1.6 %products.6 = (f32[2,1024,128]{2,1,0:T(8,128)S(1)}, s32[1032,128]{1,0:T(8,128)S(1)}) custom-call(bf16[2,1024,1024]{2,1,0:T(8,128)(2,1)S(1)} %get-tuple-element.27.weights, bf16[1024,256]{1,0:T(8,128)(2,1)S(1)} %get-tuple-element.28.refs_0_, bf16[1024,256]{1,0:T(8,128)(2,1)S(1)} %collective-permute-done.refs_1_, ...), custom_call_target="tpu_custom_call" | custom-call | flops 1073741824 | bytes 7868416 | tf_op jit(solution)/shard_map/products/pallas_call | solution.py:83
  30.3 1.8 %collective-permute-done.11.refs_1_ = bf16[2,1024,128]{2,1,0:T(8,128)(2,1)S(1)} collective-permute-done((bf16[2,1024,128]{2,1,0:T(8,128)(2,1)S(1)}, bf16[2,1024,128]{2,1,0:T(8,128)(2,1)S(1)}, u32[]{:S(2)}, u32[]{:S(2)}) %collective-permute-start.11) | collective-permute-done | bytes 524320 | tf_op jit(solution)/shard_map/ppermute | solution.py:266
  33.7 4.3 %collective-permute-start.18 = (bf16[2,1024,128]{2,1,0:T(8,128)(2,1)S(1)}, bf16[2,1024,128]{2,1,0:T(8,128)(2,1)S(1)}, u32[]{:S(2)}, u32[]{:S(2)}) collective-permute-start(bf16[2,1024,128]{2,1,0:T(8,128)(2,1)S(1)} %collective-permute-done.11.refs_1_), channel_id=1, source_target_pairs={{0,6},{1,7},{2,0},{3,1},{4,2},{5,3},{6,4},{7,5},{8,14},{9,15},{10,... | collective-permute-start | bytes 1572872 | tf_op jit(solution)/shard_map/ppermute | solution.py:266
  39.7 3.7 %collective-permute-done.13.refs_2_ = bf16[2,1024,128]{2,1,0:T(8,128)(2,1)S(1)} collective-permute-done((bf16[2,1024,128]{2,1,0:T(8,128)(2,1)S(1)}, bf16[2,1024,128]{2,1,0:T(8,128)(2,1)S(1)}, u32[]{:S(2)}, u32[]{:S(2)}) %collective-permute-start.13) | collective-permute-done | bytes 524320 | tf_op jit(solution)/shard_map/ppermute | solution.py:260
  43.5 3.0 %collective-permute-done.18.refs_1_ = bf16[2,1024,128]{2,1,0:T(8,128)(2,1)S(1)} collective-permute-done((bf16[2,1024,128]{2,1,0:T(8,128)(2,1)S(1)}, bf16[2,1024,128]{2,1,0:T(8,128)(2,1)S(1)}, u32[]{:S(2)}, u32[]{:S(2)}) %collective-permute-start.18) | collective-permute-done | bytes 524320 | tf_op jit(solution)/shard_map/ppermute | solution.py:266
  48.5 4.3 %collective-permute-start.10 = (s32[520,128]{1,0:T(8,128)S(1)}, s32[520,128]{1,0:T(8,128)S(1)}, u32[]{:S(2)}, u32[]{:S(2)}) collective-permute-start(s32[520,128]{1,0:T(8,128)S(1)} %partial_sums.3), channel_id=1, source_target_pairs={{0,6},{1,7},{2,0},{3,1},{4,2},{5,3},{6,4},{7,5},{8,14},{9,15},{10,... | collective-permute-start | bytes 798728 | tf_op jit(solution)/shard_map/ppermute | solution.py:266
  54.4 4.5 %collective-permute-done.10.refs_0_ = s32[520,128]{1,0:T(8,128)S(1)} collective-permute-done((s32[520,128]{1,0:T(8,128)S(1)}, s32[520,128]{1,0:T(8,128)S(1)}, u32[]{:S(2)}, u32[]{:S(2)}) %collective-permute-start.10) | collective-permute-done | bytes 266272 | tf_op jit(solution)/shard_map/ppermute | solution.py:266
  58.9 1.6 %partial_sums.4 = s32[520,128]{1,0:T(8,128)S(1)} custom-call(s32[4,8]{1,0:T(4,128)S(1)} %copy-done.4, f32[2,1024,128]{2,1,0:T(8,128)S(1)} %get-tuple-element.39.kept, s32[1032,128]{1,0:T(8,128)S(1)} %collective-permute-done.4.received, s32[520,128]{1,0:T(8,128)S(1)} %collective-permute-done.10.refs_0_, ...), custom_call_target="tpu_custom_call" | custom-call | flops 2097152 | bytes 4206720 | tf_op jit(solution)/shard_map/partial_sums/pallas_call | solution.py:83
  61.1 4.3 %collective-permute-start.17 = (s32[520,128]{1,0:T(8,128)S(1)}, s32[520,128]{1,0:T(8,128)S(1)}, u32[]{:S(2)}, u32[]{:S(2)}) collective-permute-start(s32[520,128]{1,0:T(8,128)S(1)} %partial_sums.4), channel_id=1, source_target_pairs={{0,6},{1,7},{2,0},{3,1},{4,2},{5,3},{6,4},{7,5},{8,14},{9,15},{10,... | collective-permute-start | bytes 798728 | tf_op jit(solution)/shard_map/ppermute | solution.py:266
  69.7 1.7 %collective-permute-done.17.refs_0_ = s32[520,128]{1,0:T(8,128)S(1)} collective-permute-done((s32[520,128]{1,0:T(8,128)S(1)}, s32[520,128]{1,0:T(8,128)S(1)}, u32[]{:S(2)}, u32[]{:S(2)}) %collective-permute-start.17) | collective-permute-done | bytes 266272 | tf_op jit(solution)/shard_map/ppermute | solution.py:266
  71.4 1.6 %partial_sums.5 = s32[520,128]{1,0:T(8,128)S(1)} custom-call(s32[4,8]{1,0:T(4,128)S(1)} %copy-done.4, f32[2,1024,128]{2,1,0:T(8,128)S(1)} %get-tuple-element.42.kept, s32[1032,128]{1,0:T(8,128)S(1)} %collective-permute-done.9.received, s32[520,128]{1,0:T(8,128)S(1)} %collective-permute-done.17.refs_0_, ...), custom_call_target="tpu_custom_call" | custom-call | flops 2097152 | bytes 4206720 | tf_op jit(solution)/shard_map/partial_sums/pallas_call | solution.py:83
  73.0 4.3 %collective-permute-start.22 = (s32[520,128]{1,0:T(8,128)S(1)}, s32[520,128]{1,0:T(8,128)S(1)}, u32[]{:S(2)}, u32[]{:S(2)}) collective-permute-start(s32[520,128]{1,0:T(8,128)S(1)} %partial_sums.5), channel_id=1, source_target_pairs={{0,6},{1,7},{2,0},{3,1},{4,2},{5,3},{6,4},{7,5},{8,14},{9,15},{10,... | collective-permute-start | bytes 798728 | tf_op jit(solution)/shard_map/ppermute | solution.py:266
  77.4 3.5 %collective-permute-done.23.refs_2_ = bf16[2,1024,128]{2,1,0:T(8,128)(2,1)S(1)} collective-permute-done((bf16[2,1024,128]{2,1,0:T(8,128)(2,1)S(1)}, bf16[2,1024,128]{2,1,0:T(8,128)(2,1)S(1)}, u32[]{:S(2)}, u32[]{:S(2)}) %collective-permute-start.23) | collective-permute-done | bytes 524320 | tf_op jit(solution)/shard_map/ppermute | solution.py:260
  80.9 1.7 %collective-permute-done.22.refs_0_ = s32[520,128]{1,0:T(8,128)S(1)} collective-permute-done((s32[520,128]{1,0:T(8,128)S(1)}, s32[520,128]{1,0:T(8,128)S(1)}, u32[]{:S(2)}, u32[]{:S(2)}) %collective-permute-start.22) | collective-permute-done | bytes 266272 | tf_op jit(solution)/shard_map/ppermute | solution.py:266
  82.8 1.7 %collective-permute-done.24.refs_4_ = bf16[2,1024,128]{2,1,0:T(8,128)(2,1)S(1)} collective-permute-done((bf16[2,1024,128]{2,1,0:T(8,128)(2,1)S(1)}, bf16[2,1024,128]{2,1,0:T(8,128)(2,1)S(1)}, u32[]{:S(2)}, u32[]{:S(2)}) %collective-permute-start.24) | collective-permute-done | bytes 524320 | tf_op jit(solution)/shard_map/ppermute | solution.py:257
  84.5 1.9 %final_sums.1 = bf16[1024,128]{1,0:T(8,128)(2,1)} custom-call(s32[4,8]{1,0:T(4,128)S(1)} %copy-done.4, f32[2,1024,128]{2,1,0:T(8,128)S(1)} %get-tuple-element.30.kept, f32[2,1024,128]{2,1,0:T(8,128)S(1)} %unpacked_products.1.received, s32[520,128]{1,0:T(8,128)S(1)} %collective-permute-done.22.refs_0_, bf16[2,1024,128]{2,1,0:T(8,128)(2,1)S(1)} %get-tuple-element.46.refs_1_, ...), custom_call_target="tpu_custom_call" | custom-call | flops 2097152 | bytes 4722816 | tf_op jit(solution)/shard_map/final_sums/pallas_call | solution.py:83
  (46 shorter events, 18.5 us)
Async XLA Ops:
  0.0 15.1 %collective-permute-start = (bf16[1024,256]{1,0:T(8,128)(2,1)}, bf16[1024,256]{1,0:T(8,128)(2,1)S(1)}, u32[]{:S(2)}, u32[]{:S(2)}) collective-permute-start(bf16[1024,256]{1,0:T(8,128)(2,1)} %refs_1_.1), channel_id=1, source_target_pairs={{0,16},{8,24},{16,0},{24,8},{1,17},{9,25},{17,1},{25,9},{2,18},{10... | collective-permute-start | bytes 1572872 | tf_op jit(solution)/shard_map/ppermute | solution.py:260
  2.9 14.8 %collective-permute-start.5 = (bf16[2,1024,128]{2,1,0:T(8,128)(2,1)}, bf16[2,1024,128]{2,1,0:T(8,128)(2,1)S(1)}, u32[]{:S(2)}, u32[]{:S(2)}) collective-permute-start(bf16[2,1024,128]{2,1,0:T(8,128)(2,1)} %refs_2_.1), channel_id=1, source_target_pairs={{0,6},{1,7},{2,0},{3,1},{4,2},{5,3},{6,4},{7,5},{8,14},{9,15},{10,... | collective-permute-start | bytes 1572872 | tf_op jit(solution)/shard_map/ppermute | solution.py:266
  6.5 15.9 %collective-permute-start.1 = (bf16[1024,256]{1,0:T(8,128)(2,1)}, bf16[1024,256]{1,0:T(8,128)(2,1)S(1)}, u32[]{:S(2)}, u32[]{:S(2)}) collective-permute-start(bf16[1024,256]{1,0:T(8,128)(2,1)} %refs_1_.1), channel_id=1, source_target_pairs={{0,8},{8,0},{16,24},{24,16},{1,9},{9,1},{17,25},{25,17},{2,10},{10... | collective-permute-start | bytes 1572872 | tf_op jit(solution)/shard_map/ppermute | solution.py:257
  15.1 7.4 %collective-permute-start.2 = (bf16[1024,256]{1,0:T(8,128)(2,1)S(1)}, bf16[1024,256]{1,0:T(8,128)(2,1)S(1)}, u32[]{:S(2)}, u32[]{:S(2)}) collective-permute-start(bf16[1024,256]{1,0:T(8,128)(2,1)S(1)} %collective-permute-done.refs_1_), channel_id=1, source_target_pairs={{0,8},{8,0},{16,24},{24,16},{1,9},{9,1},{17,25},{25,17},{2,10},{10... | collective-permute-start | bytes 1572872 | tf_op jit(solution)/shard_map/ppermute | solution.py:257
  15.1 15.2 %collective-permute-start.12 = (bf16[2,1024,128]{2,1,0:T(8,128)(2,1)S(1)}, bf16[2,1024,128]{2,1,0:T(8,128)(2,1)S(1)}, u32[]{:S(2)}, u32[]{:S(2)}) collective-permute-start(bf16[2,1024,128]{2,1,0:T(8,128)(2,1)S(1)} %copy-done.2), channel_id=1, source_target_pairs={{0,8},{8,0},{16,24},{24,16},{1,9},{9,1},{17,25},{25,17},{2,10},{10... | collective-permute-start | bytes 1572872 | tf_op jit(solution)/shard_map/ppermute | solution.py:257
  17.8 12.6 %collective-permute-start.6 = (bf16[2,1024,128]{2,1,0:T(8,128)(2,1)S(1)}, bf16[2,1024,128]{2,1,0:T(8,128)(2,1)S(1)}, u32[]{:S(2)}, u32[]{:S(2)}) collective-permute-start(bf16[2,1024,128]{2,1,0:T(8,128)(2,1)S(1)} %collective-permute-done.5.refs_0_), channel_id=1, source_target_pairs={{0,16},{8,24},{16,0},{24,8},{1,17},{9,25},{17,1},{25,9},{2,18},{10... | collective-permute-start | bytes 1572872 | tf_op jit(solution)/shard_map/ppermute | solution.py:260
  18.3 13.9 %collective-permute-start.11 = (bf16[2,1024,128]{2,1,0:T(8,128)(2,1)S(1)}, bf16[2,1024,128]{2,1,0:T(8,128)(2,1)S(1)}, u32[]{:S(2)}, u32[]{:S(2)}) collective-permute-start(bf16[2,1024,128]{2,1,0:T(8,128)(2,1)S(1)} %collective-permute-done.5.refs_0_), channel_id=1, source_target_pairs={{0,6},{1,7},{2,0},{3,1},{4,2},{5,3},{6,4},{7,5},{8,14},{9,15},{10,... | collective-permute-start | bytes 1572872 | tf_op jit(solution)/shard_map/ppermute | solution.py:266
  24.0 14.0 %collective-permute-start.3 = (s32[1032,128]{1,0:T(8,128)S(1)}, s32[1032,128]{1,0:T(8,128)S(1)}, u32[]{:S(2)}, u32[]{:S(2)}) collective-permute-start(s32[1032,128]{1,0:T(8,128)S(1)} %get-tuple-element.34), channel_id=1, source_target_pairs={{0,1},{1,0},{2,3},{3,2},{4,5},{5,4},{6,7},{7,6},{8,9},{9,8},{10,11... | collective-permute-start | bytes 1585160 | tf_op jit(solution)/shard_map/ppermute | solution.py:263
  32.2 11.3 %collective-permute-start.13 = (bf16[2,1024,128]{2,1,0:T(8,128)(2,1)S(1)}, bf16[2,1024,128]{2,1,0:T(8,128)(2,1)S(1)}, u32[]{:S(2)}, u32[]{:S(2)}) collective-permute-start(bf16[2,1024,128]{2,1,0:T(8,128)(2,1)S(1)} %collective-permute-done.11.refs_1_), channel_id=1, source_target_pairs={{0,16},{8,24},{16,0},{24,8},{1,17},{9,25},{17,1},{25,9},{2,18},{10... | collective-permute-start | bytes 1572872 | tf_op jit(solution)/shard_map/ppermute | solution.py:260
  33.7 12.8 %collective-permute-start.18 = (bf16[2,1024,128]{2,1,0:T(8,128)(2,1)S(1)}, bf16[2,1024,128]{2,1,0:T(8,128)(2,1)S(1)}, u32[]{:S(2)}, u32[]{:S(2)}) collective-permute-start(bf16[2,1024,128]{2,1,0:T(8,128)(2,1)S(1)} %collective-permute-done.11.refs_1_), channel_id=1, source_target_pairs={{0,6},{1,7},{2,0},{3,1},{4,2},{5,3},{6,4},{7,5},{8,14},{9,15},{10,... | collective-permute-start | bytes 1572872 | tf_op jit(solution)/shard_map/ppermute | solution.py:266
  38.0 8.5 %collective-permute-start.7 = (bf16[2,1024,128]{2,1,0:T(8,128)(2,1)S(1)}, bf16[2,1024,128]{2,1,0:T(8,128)(2,1)S(1)}, u32[]{:S(2)}, u32[]{:S(2)}) collective-permute-start(bf16[2,1024,128]{2,1,0:T(8,128)(2,1)S(1)} %collective-permute-done.5.refs_0_), channel_id=1, source_target_pairs={{0,8},{8,0},{16,24},{24,16},{1,9},{9,1},{17,25},{25,17},{2,10},{10... | collective-permute-start | bytes 1572872 | tf_op jit(solution)/shard_map/ppermute | solution.py:257
  38.0 14.9 %collective-permute-start.4 = (s32[1032,128]{1,0:T(8,128)S(1)}, s32[1032,128]{1,0:T(8,128)S(1)}, u32[]{:S(2)}, u32[]{:S(2)}) collective-permute-start(s32[1032,128]{1,0:T(8,128)S(1)} %get-tuple-element.35), channel_id=1, source_target_pairs={{0,1},{1,0},{2,3},{3,2},{4,5},{5,4},{6,7},{7,6},{8,9},{9,8},{10,11... | collective-permute-start | bytes 1585160 | tf_op jit(solution)/shard_map/ppermute | solution.py:263
  39.5 7.5 %collective-permute-start.8 = (bf16[2,1024,128]{2,1,0:T(8,128)(2,1)S(1)}, bf16[2,1024,128]{2,1,0:T(8,128)(2,1)S(1)}, u32[]{:S(2)}, u32[]{:S(2)}) collective-permute-start(bf16[2,1024,128]{2,1,0:T(8,128)(2,1)S(1)} %collective-permute-done.6.refs_1_), channel_id=1, source_target_pairs={{0,8},{8,0},{16,24},{24,16},{1,9},{9,1},{17,25},{25,17},{2,10},{10... | collective-permute-start | bytes 1572872 | tf_op jit(solution)/shard_map/ppermute | solution.py:257
  43.5 10.9 %collective-permute-start.14 = (bf16[2,1024,128]{2,1,0:T(8,128)(2,1)S(1)}, bf16[2,1024,128]{2,1,0:T(8,128)(2,1)S(1)}, u32[]{:S(2)}, u32[]{:S(2)}) collective-permute-start(bf16[2,1024,128]{2,1,0:T(8,128)(2,1)S(1)} %collective-permute-done.11.refs_1_), channel_id=1, source_target_pairs={{0,8},{8,0},{16,24},{24,16},{1,9},{9,1},{17,25},{25,17},{2,10},{10... | collective-permute-start | bytes 1572872 | tf_op jit(solution)/shard_map/ppermute | solution.py:257
  46.5 12.4 %collective-permute-start.15 = (bf16[2,1024,128]{2,1,0:T(8,128)(2,1)S(1)}, bf16[2,1024,128]{2,1,0:T(8,128)(2,1)S(1)}, u32[]{:S(2)}, u32[]{:S(2)}) collective-permute-start(bf16[2,1024,128]{2,1,0:T(8,128)(2,1)S(1)} %collective-permute-done.13.refs_2_), channel_id=1, source_target_pairs={{0,8},{8,0},{16,24},{24,16},{1,9},{9,1},{17,25},{25,17},{2,10},{10... | collective-permute-start | bytes 1572872 | tf_op jit(solution)/shard_map/ppermute | solution.py:257
  46.5 14.3 %collective-permute-start.19 = (bf16[2,1024,128]{2,1,0:T(8,128)(2,1)S(1)}, bf16[2,1024,128]{2,1,0:T(8,128)(2,1)S(1)}, u32[]{:S(2)}, u32[]{:S(2)}) collective-permute-start(bf16[2,1024,128]{2,1,0:T(8,128)(2,1)S(1)} %collective-permute-done.18.refs_1_), channel_id=1, source_target_pairs={{0,16},{8,24},{16,0},{24,8},{1,17},{9,25},{17,1},{25,9},{2,18},{10... | collective-permute-start | bytes 1572872 | tf_op jit(solution)/shard_map/ppermute | solution.py:260
  48.5 10.4 %collective-permute-start.10 = (s32[520,128]{1,0:T(8,128)S(1)}, s32[520,128]{1,0:T(8,128)S(1)}, u32[]{:S(2)}, u32[]{:S(2)}) collective-permute-start(s32[520,128]{1,0:T(8,128)S(1)} %partial_sums.3), channel_id=1, source_target_pairs={{0,6},{1,7},{2,0},{3,1},{4,2},{5,3},{6,4},{7,5},{8,14},{9,15},{10,... | collective-permute-start | bytes 798728 | tf_op jit(solution)/shard_map/ppermute | solution.py:266
  52.9 13.9 %collective-permute-start.9 = (s32[1032,128]{1,0:T(8,128)S(1)}, s32[1032,128]{1,0:T(8,128)S(1)}, u32[]{:S(2)}, u32[]{:S(2)}) collective-permute-start(s32[1032,128]{1,0:T(8,128)S(1)} %get-tuple-element.38), channel_id=1, source_target_pairs={{0,1},{1,0},{2,3},{3,2},{4,5},{5,4},{6,7},{7,6},{8,9},{9,8},{10,11... | collective-permute-start | bytes 1585160 | tf_op jit(solution)/shard_map/ppermute | solution.py:263
  60.5 10.9 %collective-permute-start.20 = (bf16[2,1024,128]{2,1,0:T(8,128)(2,1)S(1)}, bf16[2,1024,128]{2,1,0:T(8,128)(2,1)S(1)}, u32[]{:S(2)}, u32[]{:S(2)}) collective-permute-start(bf16[2,1024,128]{2,1,0:T(8,128)(2,1)S(1)} %collective-permute-done.18.refs_1_), channel_id=1, source_target_pairs={{0,8},{8,0},{16,24},{24,16},{1,9},{9,1},{17,25},{25,17},{2,10},{10... | collective-permute-start | bytes 1572872 | tf_op jit(solution)/shard_map/ppermute | solution.py:257
  60.8 10.6 %collective-permute-start.21 = (bf16[2,1024,128]{2,1,0:T(8,128)(2,1)S(1)}, bf16[2,1024,128]{2,1,0:T(8,128)(2,1)S(1)}, u32[]{:S(2)}, u32[]{:S(2)}) collective-permute-start(bf16[2,1024,128]{2,1,0:T(8,128)(2,1)S(1)} %collective-permute-done.19.refs_2_), channel_id=1, source_target_pairs={{0,8},{8,0},{16,24},{24,16},{1,9},{9,1},{17,25},{25,17},{2,10},{10... | collective-permute-start | bytes 1572872 | tf_op jit(solution)/shard_map/ppermute | solution.py:257
  61.1 10.3 %collective-permute-start.17 = (s32[520,128]{1,0:T(8,128)S(1)}, s32[520,128]{1,0:T(8,128)S(1)}, u32[]{:S(2)}, u32[]{:S(2)}) collective-permute-start(s32[520,128]{1,0:T(8,128)S(1)} %partial_sums.4), channel_id=1, source_target_pairs={{0,6},{1,7},{2,0},{3,1},{4,2},{5,3},{6,4},{7,5},{8,14},{9,15},{10,... | collective-permute-start | bytes 798728 | tf_op jit(solution)/shard_map/ppermute | solution.py:266
  66.7 15.9 %collective-permute-start.16 = (s32[1032,128]{1,0:T(8,128)S(1)}, s32[1032,128]{1,0:T(8,128)S(1)}, u32[]{:S(2)}, u32[]{:S(2)}) collective-permute-start(s32[1032,128]{1,0:T(8,128)S(1)} %get-tuple-element.41), channel_id=1, source_target_pairs={{0,1},{1,0},{2,3},{3,2},{4,5},{5,4},{6,7},{7,6},{8,9},{9,8},{10,11... | collective-permute-start | bytes 1585160 | tf_op jit(solution)/shard_map/ppermute | solution.py:263
  68.2 12.6 %collective-permute-start.23 = (bf16[2,1024,128]{2,1,0:T(8,128)(2,1)S(1)}, bf16[2,1024,128]{2,1,0:T(8,128)(2,1)S(1)}, u32[]{:S(2)}, u32[]{:S(2)}) collective-permute-start(bf16[2,1024,128]{2,1,0:T(8,128)(2,1)S(1)} %copy-done.3), channel_id=1, source_target_pairs={{0,16},{8,24},{16,0},{24,8},{1,17},{9,25},{17,1},{25,9},{2,18},{10... | collective-permute-start | bytes 1572872 | tf_op jit(solution)/shard_map/ppermute | solution.py:260
  73.0 9.6 %collective-permute-start.22 = (s32[520,128]{1,0:T(8,128)S(1)}, s32[520,128]{1,0:T(8,128)S(1)}, u32[]{:S(2)}, u32[]{:S(2)}) collective-permute-start(s32[520,128]{1,0:T(8,128)S(1)} %partial_sums.5), channel_id=1, source_target_pairs={{0,6},{1,7},{2,0},{3,1},{4,2},{5,3},{6,4},{7,5},{8,14},{9,15},{10,... | collective-permute-start | bytes 798728 | tf_op jit(solution)/shard_map/ppermute | solution.py:266
  (6 other events, 62.4 us)
